TPU v7x, 256 devices: a whole 4x4x8 slice. The times are simulated.
256 devices in a mesh: seq: 64 (over x, y_hi, z), head: 4 (over y_lo, core).
Axes of the slice: x: 4, y: 4 (y_hi: 2, y_lo: 2; y = y_hi * 2 + y_lo), z: 8, core: 2. Of those that a mesh axis runs over, the one named last changes fastest.
Arguments:
- queries: bfloat16 [131072, 2048], P('seq', 'head'), may hold values from -6 to 6
- keys: bfloat16 [131072, 2048], P('seq', 'head'), may hold values from -6 to 6
- values: bfloat16 [131072, 2048], P('seq', 'head'), may hold values from -6 to 6
- out_weight: bfloat16 [2048, 2048], P('head'), may hold values from -0.125 to 0.125
Outputs:
- mixed: bfloat16 [131072, 2048], P(('seq', 'head'))
All inputs are finite; a program needn't handle non-finite values.
Results may differ from a plain program's by a relative error of at most 0.0051.
Values may be sent and summed in bfloat16 or wider, within the bound.
No kernel may reach another device: no remote copies, remote signals or barrier semaphores. Data moves between devices by JAX's collectives and lax.ppermute only.
A program may use at most 128 MiB of HBM per device.

v0:
```python
import jax
import jax.numpy as jnp
from jax import lax
from jax.sharding import PartitionSpec as P

HD = 128


def with_halo(block, sides, width):
    for axis, dim in sides:
        count = lax.axis_size(axis)
        forward = [(i, i + 1) for i in range(count - 1)]
        backward = [(target, source) for source, target in forward]
        low = lax.ppermute(
            lax.slice_in_dim(block, block.shape[dim] - width, None, axis=dim), axis, forward
        )
        high = lax.ppermute(lax.slice_in_dim(block, 0, width, axis=dim), axis, backward)
        block = jnp.concatenate([low, block, high], axis=dim)
    return block


def pooled(stack, size):
    shaped = stack.astype(jnp.float32).reshape(stack.shape[0], -1, size, stack.shape[2])
    return jnp.mean(shaped, axis=2).astype(jnp.bfloat16)


def attend_block(query_block, start, fine_window, coarse_window, middle_window, summit, total):
    rows = query_block.shape[0]
    width = query_block.shape[1]
    heads = width // HD
    positions = start + jnp.arange(rows, dtype=jnp.int32)
    fine_block = positions // 16
    first_level = positions // 256
    second_level = positions // 4096
    near_tokens = start - 16 + jnp.arange(rows + 32, dtype=jnp.int32)
    near_mask = (
        (jnp.abs(near_tokens[None, :] // 16 - fine_block[:, None]) <= 1)
        & (near_tokens[None, :] >= 0)
        & (near_tokens[None, :] < total)
    )
    level_one = start // 16 - 16 + jnp.arange(rows // 16 + 32, dtype=jnp.int32)
    one_mask = (
        (jnp.abs(level_one[None, :] // 16 - first_level[:, None]) <= 1)
        & (jnp.abs(level_one[None, :] - fine_block[:, None]) > 1)
        & (level_one[None, :] >= 0)
        & (level_one[None, :] < total // 16)
    )
    level_two = 16 * (start // 4096) - 16 + jnp.arange(48, dtype=jnp.int32)
    two_mask = (
        (jnp.abs(level_two[None, :] // 16 - second_level[:, None]) <= 1)
        & (jnp.abs(level_two[None, :] - first_level[:, None]) > 1)
        & (level_two[None, :] >= 0)
        & (level_two[None, :] < total // 256)
    )
    level_three = jnp.arange(summit.shape[1], dtype=jnp.int32)
    three_mask = jnp.abs(level_three[None, :] - second_level[:, None]) > 1
    mask = jnp.concatenate([near_mask, one_mask, two_mask, three_mask], axis=1)
    key_rows = jnp.concatenate(
        [fine_window[0], coarse_window[0], middle_window[0], summit[0]], axis=0
    ).reshape(-1, heads, HD)
    value_rows = jnp.concatenate(
        [fine_window[1], coarse_window[1], middle_window[1], summit[1]], axis=0
    ).reshape(-1, heads, HD)
    query_heads = query_block.reshape(rows, heads, HD)
    scores = jnp.einsum(
        "rhd,khd->hrk", query_heads, key_rows, preferred_element_type=jnp.float32
    ) * HD ** (-0.5)
    scores = jnp.where(mask[None], scores, -jnp.inf)
    peak = jnp.max(scores, axis=2, keepdims=True)
    expo = jnp.where(mask[None], jnp.exp(scores - peak), 0.0)
    totals = jnp.sum(expo, axis=2)
    weights = expo.astype(jnp.bfloat16)
    summed = jnp.einsum("hrk,khd->rhd", weights, value_rows, preferred_element_type=jnp.float32)
    return (summed / jnp.transpose(totals)[:, :, None]).astype(jnp.bfloat16).reshape(rows, width)


def body(queries, keys, values, out_weight):
    rows_dev = queries.shape[0]
    width = queries.shape[1]
    first_token = lax.axis_index("seq") * rows_dev
    total = rows_dev * lax.axis_size("seq")
    stack = jnp.stack([keys, values])
    fine_pad = with_halo(stack, (("seq", 1),), 16)
    coarse_pad = with_halo(pooled(stack, 16), (("seq", 1),), 16)
    middle = lax.all_gather(pooled(stack, 256), "seq", axis=1, tiled=True)
    summit = pooled(middle, 16)
    middle_pad = jnp.pad(middle, ((0, 0), (16, 16), (0, 0)))

    def one_block(index):
        offset = index * 512
        start = first_token + offset
        query_block = lax.dynamic_slice_in_dim(queries, offset, 512, 0)
        fine_window = lax.dynamic_slice_in_dim(fine_pad, offset, 544, 1)
        coarse_window = lax.dynamic_slice_in_dim(coarse_pad, offset // 16, 64, 1)
        middle_window = lax.dynamic_slice_in_dim(middle_pad, 16 * (start // 4096), 48, 1)
        return attend_block(
            query_block, start, fine_window, coarse_window, middle_window, summit, total
        )

    attended = lax.map(one_block, jnp.arange(rows_dev // 512, dtype=jnp.int32)).reshape(
        rows_dev, width
    )
    result = lax.psum_scatter(
        jnp.dot(attended, out_weight, preferred_element_type=jnp.float32),
        "head",
        scatter_dimension=0,
        tiled=True,
    )
    return result.astype(jnp.bfloat16)


def solution(mesh):
    placed = (P("seq", "head"), P("seq", "head"), P("seq", "head"), P("head", None))
    return jax.shard_map(
        body, mesh=mesh, in_specs=placed, out_specs=P(("seq", "head"), None), check_vma=False
    )
```

profile of v0, /device:TPU:1, one launch (start us, length us, event | category | flops | bytes accessed | tf_op | source)
XLA Modules:
  0.0 366.9 jit_solution(10499603588049754614)
XLA Ops:
  6.5 3.0 convert_reduce_fusion
  10.2 4.6 %convert_reduce_fusion.1 = f32[2,128,512]{2,1,0:T(8,128)S(1)} fusion(bf16[1,128,16,512]{3,2,1,0:T(8,128)(2,1)} %bitcast.40, bf16[1,128,16,512]{3,2,1,0:T(8,128)(2,1)} %bitcast.44), kind=kLoop, calls=%fused_computation.99 | loop fusion | flops 6160384 | bytes 4718592 | tf_op jit(solution)/shard_map/reduce_sum | solution.py:24
  14.9 4.4 %collective-permute-start.2 = (bf16[2,16,512]{2,1,0:T(8,128)(2,1)S(1)}, bf16[2,16,512]{2,1,0:T(8,128)(2,1)S(1)}, u32[]{:S(2)}, u32[]{:S(2)}) collective-permute-start(bf16[2,16,512]{2,1,0:T(8,128)(2,1)S(1)} %get-tuple-element.215), channel_id=1, source_target_pairs={{0,4},{4,8},{8,12},{12,16},{16,20},{20,24},{24,28},{28,32},{32,36}... | collective-permute-start | bytes 98312 | tf_op jit(solution)/shard_map/ppermute | solution.py:14
  19.3 1.3 collective-permute-start.3
  20.6 4.2 %collective-permute-start = (bf16[2,16,512]{2,1,0:T(8,128)(2,1)S(1)}, bf16[2,16,512]{2,1,0:T(8,128)(2,1)S(1)}, u32[]{:S(2)}, u32[]{:S(2)}) collective-permute-start(bf16[2,16,512]{2,1,0:T(8,128)(2,1)S(1)} %get-tuple-element.213), channel_id=1, source_target_pairs={{0,4},{4,8},{8,12},{12,16},{16,20},{20,24},{24,28},{28,32},{32,36}... | collective-permute-start | bytes 98312 | tf_op jit(solution)/shard_map/ppermute | solution.py:14
  24.8 1.3 collective-permute-start.1
  26.9 2.8 collective-permute-done.1
  29.6 3.7 %pad_maximum_fusion = bf16[2,2080,512]{2,1,0:T(8,128)(2,1)} fusion(bf16[2,16,512]{2,1,0:T(8,128)(2,1)S(1)} %collective-permute-done.1, bf16[1,2048,512]{2,1,0:T(8,128)(2,1)} %bitcast.41, bf16[1,2048,512]{2,1,0:T(8,128)(2,1)} %bitcast.45, bf16[2,16,512]{2,1,0:T(8,128)(2,1)S(1)} %collective-permute-done), kind=kLoop, calls=%fused_computation.100 | loop fusion | flops 17039360 | bytes 8519680 | tf_op jit(solution)/shard_map/concatenate | solution.py:18
  33.4 82.2 %all-gather.2.cloned.1.call-done = bf16[2,512,512]{2,1,0:T(8,128)(2,1)} async-done(((bf16[2,8,512]{2,1,0:T(8,128)(2,1)}), bf16[2,512,512]{2,1,0:T(8,128)(2,1)}) %all-gather.2.cloned.1.call-update) | async-done | bytes 1048592 | tf_op jit(solution)/shard_map/all_gather | solution.py:85
  115.5 1.7 convert_reduce_fusion.2
  118.3 77.6 %while.13 = (s32[]{:T(128)}, bf16[4,512,512]{2,1,0:T(8,128)(2,1)}, s32[4]{0:T(128)S(1)}, bf16[2,2080,512]{2,1,0:T(8,128)(2,1)}, bf16[2,160,512]{2,1,0:T(8,128)(2...) while((s32[]{:T(128)}, bf16[4,512,512]{2,1,0:T(8,128)(2,1)}, ...), condition=%wide.region_6.7_spmd, body=%wide.region_3.6_spmd.sunk | while | flops 741902208 | bytes 35007996 | solution.py:100
  124.1 1.1 constant_dynamic-slice_fusion.11
  126.2 1.3 constant_dynamic-slice_fusion.14
  128.5 1.9 copy.35
  130.6 2.1 fusion.80
  132.8 3.2 fusion.85
  143.5 1.1 constant_dynamic-slice_fusion.11
  145.6 1.3 constant_dynamic-slice_fusion.14
  147.9 1.9 copy.35
  150.0 2.1 fusion.80
  152.2 3.2 fusion.85
  165.0 1.3 constant_dynamic-slice_fusion.14
  167.3 1.9 copy.35
  169.5 2.1 fusion.80
  171.6 3.2 fusion.85
  184.4 1.3 constant_dynamic-slice_fusion.14
  186.6 1.9 copy.35
  188.8 2.1 fusion.80
  191.0 3.2 fusion.85
  195.9 9.7 %fusion.58 = f32[2048,2048]{1,0:T(8,128)} fusion(bf16[2048,512]{1,0:T(8,128)(2,1)} %bitcast.48, bf16[512,2048]{1,0:T(8,128)(2,1)S(1)} %copy-done), kind=kOutput, calls=%fused_computation.111 | convolution fusion | flops 4294967296 | bytes 20971520 | tf_op jit(solution)/shard_map/dot_general | solution.py:104
  205.7 150.5 %reduce-scatter.2.cloned.1.call-done = f32[512,2048]{1,0:T(8,128)} async-done(((f32[2048,2048]{1,0:T(8,128)}), f32[512,2048]{1,0:T(8,128)}) %reduce-scatter.2.cloned.1.call-update) | async-done | bytes 4194320 | tf_op jit(solution)/shard_map/reduce_scatter | solution.py:103
  356.2 3.8 %convert_element_type.42 = bf16[512,2048]{1,0:T(8,128)(2,1)} convert(f32[512,2048]{1,0:T(8,128)} %reduce-scatter.2.cloned.1.call-done) | non-fusion elementwise | flops 1048576 | bytes 6291456 | tf_op jit(solution)/shard_map/convert_element_type | solution.py:109
  (186 shorter events, 39.6 us)
Async XLA Ops:
  6.5 189.4 %copy-start = (bf16[512,2048]{1,0:T(8,128)(2,1)S(1)}, bf16[512,2048]{1,0:T(8,128)(2,1)}, u32[]{:S(2)}) copy-start(bf16[512,2048]{1,0:T(8,128)(2,1)} %param.9) | copy-start | bytes 6291460
  6.5 109.0 %all-gather.2.cloned.1.call-start = ((), (), s32[]{:S(2)}) async-start(), calls=%async_computation.1 | async-start | bytes 1064960 | tf_op jit(solution)/shard_map/all_gather | solution.py:85
  10.1 346.1 %reduce-scatter.2.cloned.1.call-start = ((), (), s32[]{:S(2)}) async-start(), calls=%async_computation.2 | async-start | bytes 20971520 | tf_op jit(solution)/shard_map/reduce_scatter | solution.py:103
  10.2 10.4 %copy-start.1 = (bf16[2048,512]{1,0:T(8,128)(2,1)S(1)}, bf16[2048,512]{1,0:T(8,128)(2,1)}, u32[]{:S(2)}) copy-start(bf16[2048,512]{1,0:T(8,128)(2,1)} %param.8) | copy-start | bytes 6291460
  10.2 10.4 %copy-start.2 = (bf16[2048,512]{1,0:T(8,128)(2,1)S(1)}, bf16[2048,512]{1,0:T(8,128)(2,1)}, u32[]{:S(2)}) copy-start(bf16[2048,512]{1,0:T(8,128)(2,1)} %param.7) | copy-start | bytes 6291460
  14.9 11.2 %collective-permute-start.2 = (bf16[2,16,512]{2,1,0:T(8,128)(2,1)S(1)}, bf16[2,16,512]{2,1,0:T(8,128)(2,1)S(1)}, u32[]{:S(2)}, u32[]{:S(2)}) collective-permute-start(bf16[2,16,512]{2,1,0:T(8,128)(2,1)S(1)} %get-tuple-element.215), channel_id=1, source_target_pairs={{0,4},{4,8},{8,12},{12,16},{16,20},{20,24},{24,28},{28,32},{32,36}... | collective-permute-start | bytes 98312 | tf_op jit(solution)/shard_map/ppermute | solution.py:14
  19.3 6.8 %collective-permute-start.3 = (bf16[2,16,512]{2,1,0:T(8,128)(2,1)S(1)}, bf16[2,16,512]{2,1,0:T(8,128)(2,1)S(1)}, u32[]{:S(2)}, u32[]{:S(2)}) collective-permute-start(bf16[2,16,512]{2,1,0:T(8,128)(2,1)S(1)} %get-tuple-element.216), channel_id=1, source_target_pairs={{4,0},{8,4},{12,8},{16,12},{20,16},{24,20},{28,24},{32,28},{36,32}... | collective-permute-start | bytes 98312 | tf_op jit(solution)/shard_map/ppermute | solution.py:17
  20.6 6.3 %collective-permute-start = (bf16[2,16,512]{2,1,0:T(8,128)(2,1)S(1)}, bf16[2,16,512]{2,1,0:T(8,128)(2,1)S(1)}, u32[]{:S(2)}, u32[]{:S(2)}) collective-permute-start(bf16[2,16,512]{2,1,0:T(8,128)(2,1)S(1)} %get-tuple-element.213), channel_id=1, source_target_pairs={{0,4},{4,8},{8,12},{12,16},{16,20},{20,24},{24,28},{28,32},{32,36}... | collective-permute-start | bytes 98312 | tf_op jit(solution)/shard_map/ppermute | solution.py:14
  24.8 4.8 %collective-permute-start.1 = (bf16[2,16,512]{2,1,0:T(8,128)(2,1)S(1)}, bf16[2,16,512]{2,1,0:T(8,128)(2,1)S(1)}, u32[]{:S(2)}, u32[]{:S(2)}) collective-permute-start(bf16[2,16,512]{2,1,0:T(8,128)(2,1)S(1)} %get-tuple-element.214), channel_id=1, source_target_pairs={{4,0},{8,4},{12,8},{16,12},{20,16},{24,20},{28,24},{32,28},{36,32}... | collective-permute-start | bytes 98312 | tf_op jit(solution)/shard_map/ppermute | solution.py:17
  115.5 1.7 copy-start.4
  130.6 2.2 copy-start.3
  132.8 3.3 copy-start.5
  150.0 2.1 copy-start.3
  152.2 3.3 copy-start.5
  169.4 2.1 copy-start.3
  171.6 3.3 copy-start.5
  188.8 2.1 copy-start.3
  191.0 3.3 copy-start.5
Sparse Core Ops, SparseCore 0:
  10.8 104.6 all-gather.1
  205.8 150.3 reduce-scatter.1
where the time goes:
time: 368 us; the launch traced here: 367 us
  waiting for transfers between devices  236 us (64%)
  local copies, waits for them, and re-layouts  44.1 us (12%)
  other arithmetic  37.7 us (10%)
  matrix products  20.9 us (6%)
  between operations  13.6 us (4%)
  starting transfers between devices  11.2 us (3%)
  loops' own time  3.97 us (1%)
    reduce_scatter x1, waiting for transfers between devices, body(): lax.psum_scatter(jnp.dot(attended, out_weight, preferred_element_type=jnp...  151 us
    all_gather x1, waiting for transfers between devices, body(): middle = lax.all_gather(pooled(stack, 256), 'seq', axis=1, tiled=True)  82.2 us
    sub x4, other arithmetic, attend_block(): expo = jnp.where(mask[None], jnp.exp(scores - peak), 0.0)  13 us
    concatenate x32, local copies, waits for them, and re-layouts, attend_block(): jnp.concatenate([fine_window[0], coarse_window[0], middle_window[0], summ...  11.9 us
    dot_general x1, matrix products, body(): jnp.dot(attended, out_weight, preferred_element_type=jnp.float32)  9.75 us
    reduce_sum x3, other arithmetic, pooled(): return jnp.mean(shaped, axis=2).astype(jnp.bfloat16)  9.24 us
    ppermute x2, starting transfers between devices, with_halo(): lax.ppermute(lax.slice_in_dim(block, block.shape[dim] - width, None, axis...  8.55 us
    dot_general x4, matrix products, attend_block(): jnp.einsum('rhd,khd->hrk', query_heads, key_rows, preferred_element_type=...  8.54 us
  transfers between devices with their start and end apart: 6, of which 3 were waited for; matrix products, arithmetic and copies ran while one was open for 2% of the time, Pallas kernels for 0%

commit v1 on v0

v1 whole, which is shorter than its diff:
```python
import functools

import jax
import jax.numpy as jnp
from jax import lax
from jax.experimental import pallas as pl
from jax.experimental.pallas import tpu as pltpu
from jax.sharding import PartitionSpec as P

HD = 128
HEADS = 4
WIDE = HEADS * HD
LOG2E = 1.4426950408889634
SCORE = HD**-0.5 * LOG2E
NEG = -1e30
F32 = jnp.float32
BF16 = jnp.bfloat16
VMEM_LIMIT = 48 * 1024 * 1024

TK, TV, AK, AV, BK, BV = (16 * i for i in range(6))


def mean_rows(count, size, scale):
    rows = lax.broadcasted_iota(jnp.int32, (count, count * size), 0)
    cols = lax.broadcasted_iota(jnp.int32, (count, count * size), 1)
    return jnp.where(rows == cols // size, scale, 0.0).astype(BF16)


def pool_kernel(info, k_ref, v_ref, l1_ref, near_ref, far_ref, sums):
    step = pl.program_id(0)
    odd = info[0] % 2
    ones = mean_rows(16, 16, 1.0)
    for which, ref in ((0, k_ref), (1, v_ref)):
        for part in range(2):
            block = ref[256 * part : 256 * (part + 1), :]
            total = jnp.dot(ones, block, preferred_element_type=F32)
            at = pl.multiple_of(32 * step + 16 * part, 16)
            sums[which, pl.ds(at, 16), :] = total
            l1_ref[which, 16 * part : 16 * (part + 1), :] = (total * 0.0625).astype(BF16)

    @pl.when(step == 0)
    def _():
        low = (k_ref[0:16, :], v_ref[0:16, :], l1_ref[0, 0:16, :], l1_ref[1, 0:16, :])
        for at, rows in enumerate(low):
            rows = rows.astype(BF16)

            @pl.when(odd == 1)
            def _():
                near_ref[16 * at : 16 * at + 16, :] = rows

            @pl.when(odd == 0)
            def _():
                far_ref[16 * at : 16 * at + 16, :] = rows

    @pl.when(step == pl.num_programs(0) - 1)
    def _():
        high = (k_ref[496:512, :], v_ref[496:512, :], l1_ref[0, 16:32, :], l1_ref[1, 16:32, :])
        for at, rows in enumerate(high):

            @pl.when(odd == 0)
            def _():
                near_ref[16 * at : 16 * at + 16, :] = rows

            @pl.when(odd == 1)
            def _():
                far_ref[16 * at : 16 * at + 16, :] = rows

        for which, at in ((0, BK), (1, BV)):
            means = jnp.sum(sums[which].reshape(8, 16, WIDE), axis=1) * (1.0 / 256.0)
            both = jnp.concatenate([means, means], axis=0)
            row = lax.broadcasted_iota(jnp.int32, (16, WIDE), 0)
            near_ref[at : at + 16, :] = jnp.where(row // 8 == odd, both, 0.0).astype(BF16)


def pool(info, keys, values):
    rows = keys.shape[0]
    steps = rows // 512
    return pl.pallas_call(
        pool_kernel,
        grid_spec=pltpu.PrefetchScalarGridSpec(
            num_scalar_prefetch=1,
            grid=(steps,),
            in_specs=[pl.BlockSpec((512, WIDE), lambda i, s: (i, 0))] * 2,
            out_specs=[
                pl.BlockSpec((2, 32, WIDE), lambda i, s: (0, i, 0)),
                pl.BlockSpec((96, WIDE), lambda i, s: (0, 0)),
                pl.BlockSpec((64, WIDE), lambda i, s: (0, 0)),
            ],
            scratch_shapes=[pltpu.VMEM((2, rows // 16, WIDE), F32)],
        ),
        out_shape=[
            jax.ShapeDtypeStruct((2, rows // 16, WIDE), BF16),
            jax.ShapeDtypeStruct((96, WIDE), BF16),
            jax.ShapeDtypeStruct((64, WIDE), BF16),
        ],
        cost_estimate=pl.CostEstimate(
            flops=4 * rows * 16 * WIDE, bytes_accessed=4 * rows * WIDE, transcendentals=0
        ),
        compiler_params=pltpu.CompilerParams(vmem_limit_bytes=VMEM_LIMIT),
        name="pool",
    )(info, keys, values)


def attend_kernel(
    total, info, q_ref, k_ref, kp_ref, kn_ref, v_ref, vp_ref, vn_ref, l1_ref, mid_ref, near_ref,
    far_ref, farther_ref, l3_ref, out_ref, kx, vx, l1x, sk, sv,
):
    step = pl.program_id(0)
    block = info[0]
    group = info[1 + step]
    odd = block % 2
    last_group = 2048 // 256 - 1

    @pl.when(step == 0)
    def _():
        for which, at in ((0, AK), (1, AV)):
            near, far = near_ref[at : at + 16, :], far_ref[at : at + 16, :]
            l1x[which, 0:16, :] = jnp.where(odd == 1, near, far)
            l1x[which, 16:144, :] = l1_ref[which]
            l1x[which, 144:160, :] = jnp.where(odd == 1, far, near)
        for scratch, at, which in ((sk, BK, 0), (sv, BV, 1)):
            scratch[48:64, :] = mid_ref[at - BK : at - BK + 16, :]
            scratch[64:80, :] = far_ref[at : at + 16, :]
            scratch[80:96, :] = farther_ref[at - BK : at - BK + 16, :]
            scratch[96:128, :] = l3_ref[which]
        zeros = jnp.zeros((32, WIDE), BF16)
        kx[288:320, :] = zeros
        vx[288:320, :] = zeros

    for scratch, main, before, after, at in (
        (kx, k_ref, kp_ref, kn_ref, TK),
        (vx, v_ref, vp_ref, vn_ref, TV),
    ):
        near, far = near_ref[at : at + 16, :], far_ref[at : at + 16, :]
        low = jnp.where(odd == 1, near, far)
        high = jnp.where(odd == 1, far, near)
        scratch[0:16, :] = jnp.where(group == 0, low, before[...])
        scratch[16:272, :] = main[...]
        scratch[272:288, :] = jnp.where(group == last_group, high, after[...])
    window = pl.ds(pl.multiple_of(16 * group, 16), 48)
    sk[0:48, :] = l1x[0, window, :]
    sv[0:48, :] = l1x[1, window, :]

    c = 8 * block + group
    e = block // 2
    col = lax.broadcasted_iota(jnp.int32, (64, 128), 1)
    fine = lax.broadcasted_iota(jnp.int32, (64, 128), 0) // 16
    tile = col // 16
    beside = jnp.where(odd == 0, e - 1, e + 1)
    across = jnp.where(odd == 0, e + 1, e - 1)
    m = 16 * jnp.where(tile == 3, e, jnp.where(tile == 4, beside, across)) + col % 16
    term2 = jnp.where((m >= 0) & (m < total // 256) & (jnp.abs(m - c) > 1), 0.0, NEG)
    term3 = jnp.where(jnp.abs(col - 96 - e) > 1, 0.0, NEG)
    j = 16 * (c - 1) + col
    term1 = jnp.where((j >= 0) & (j < total // 16), 0.0, NEG)
    shared = jnp.where(col < 48, term1, jnp.where(col < 96, term2, term3))
    for part in range(4):
        token = 256 * c + 64 * part - 16 + col
        ok = (jnp.abs(tile - 1 - fine) <= 1) & (token >= 0) & (token < total)
        own = (col < 48) & (jnp.abs(col - 16 - 4 * part - fine) <= 1)
        bias = jnp.concatenate(
            [jnp.where(ok, 0.0, NEG), jnp.where(own, NEG, shared)], axis=1
        ).astype(F32)
        rows = slice(64 * part, 64 * part + 64)
        near_rows = slice(64 * part, 64 * part + 128)
        for head in range(HEADS):
            cols = slice(HD * head, HD * head + HD)
            key_rows = jnp.concatenate([kx[near_rows, cols], sk[:, cols]], axis=0)
            value_rows = jnp.concatenate([vx[near_rows, cols], sv[:, cols]], axis=0)
            scores = lax.dot_general(
                q_ref[rows, cols], key_rows, (((1,), (1,)), ((), ())), preferred_element_type=F32
            )
            scores = scores * SCORE + bias
            peak = jnp.max(scores, axis=1, keepdims=True)
            expo = jnp.exp2(scores - peak)
            sums = jnp.sum(expo, axis=1, keepdims=True)
            summed = jnp.dot(expo.astype(BF16), value_rows, preferred_element_type=F32)
            out_ref[rows, cols] = (summed / sums).astype(BF16)


def attend(total, info, queries, keys, values, l1, mid, near, far, farther, l3):
    def main(i, s):
        return (s[1 + i], 0)

    def before(i, s):
        return (jnp.maximum(16 * s[1 + i] - 1, 0), 0)

    def after(i, s):
        return (jnp.minimum(16 * s[1 + i] + 16, 127), 0)

    def whole(array):
        return pl.BlockSpec(array.shape, lambda i, s: (0,) * array.ndim)

    wide, thin_low, thin_high = (
        pl.BlockSpec((256, WIDE), main),
        pl.BlockSpec((16, WIDE), before),
        pl.BlockSpec((16, WIDE), after),
    )
    small = (l1, mid, near, far, farther, l3)
    return pl.pallas_call(
        functools.partial(attend_kernel, total),
        grid_spec=pltpu.PrefetchScalarGridSpec(
            num_scalar_prefetch=1,
            grid=(2,),
            in_specs=[wide, wide, thin_low, thin_high, wide, thin_low, thin_high]
            + [whole(array) for array in small],
            out_specs=pl.BlockSpec((256, WIDE), lambda i, s: (i, 0)),
            scratch_shapes=[
                pltpu.VMEM((320, WIDE), BF16),
                pltpu.VMEM((320, WIDE), BF16),
                pltpu.VMEM((2, 160, WIDE), BF16),
                pltpu.VMEM((128, WIDE), BF16),
                pltpu.VMEM((128, WIDE), BF16),
            ],
        ),
        out_shape=jax.ShapeDtypeStruct((512, WIDE), BF16),
        cost_estimate=pl.CostEstimate(
            flops=4 * 512 * 256 * WIDE, bytes_accessed=8 * 512 * WIDE, transcendentals=512 * 256 * HEADS
        ),
        compiler_params=pltpu.CompilerParams(vmem_limit_bytes=VMEM_LIMIT),
        name="attend",
    )(info, queries, keys, keys, keys, values, values, values, *small)


def project_kernel(info, a0, a1, a2, a3, w0, w1, w2y, w2z, w3y, w3z, out_ref):
    first = pl.multiple_of(256 * info[0], 256)
    second = pl.multiple_of(256 - 256 * info[0], 256)
    total = jnp.dot(a0[...], w0[...], preferred_element_type=F32)
    total += jnp.dot(a1[...], w1[...], preferred_element_type=F32)
    for a, y, z in ((a2, w2y, w2z), (a3, w3y, w3z)):
        total += jnp.dot(a[:, pl.ds(first, 256)], y[...], preferred_element_type=F32)
        total += jnp.dot(a[:, pl.ds(second, 256)], z[...], preferred_element_type=F32)
    out_ref[...] = total.astype(BF16)


def project(info, attended, weights):
    rows, columns = attended[0].shape[0], weights[0].shape[1]
    tile = 512
    return pl.pallas_call(
        project_kernel,
        grid_spec=pltpu.PrefetchScalarGridSpec(
            num_scalar_prefetch=1,
            grid=(columns // tile,),
            in_specs=[pl.BlockSpec(a.shape, lambda i, s: (0, 0)) for a in attended]
            + [pl.BlockSpec((w.shape[0], tile), lambda i, s: (0, i)) for w in weights],
            out_specs=pl.BlockSpec((rows, tile), lambda i, s: (0, i)),
        ),
        out_shape=jax.ShapeDtypeStruct((rows, columns), BF16),
        cost_estimate=pl.CostEstimate(
            flops=2 * rows * 2048 * columns, bytes_accessed=2 * 2048 * columns, transcendentals=0
        ),
        compiler_params=pltpu.CompilerParams(vmem_limit_bytes=VMEM_LIMIT),
        name="project",
    )(info, *attended, *weights)


def body(queries, keys, values, out_weight):
    blocks = lax.axis_size("seq")
    total = queries.shape[0] * blocks
    s = lax.axis_index("seq")
    h = lax.axis_index("head")
    half = (s // 16) % 2

    def permute(array, move):
        return lax.ppermute(array, "seq", [(i, move(i) % blocks) for i in range(blocks)])

    def swap(array, bit):
        return lax.ppermute(array, "head", [(i, i ^ bit) for i in range(4)])

    w_far_y = swap(lax.dynamic_slice_in_dim(out_weight, 256 * half, 256, 0), 2)
    w_near = swap(out_weight, 1)

    l1, to_near, to_far = pool(jnp.stack([s]).astype(jnp.int32), keys, values)
    near = permute(to_near, lambda i: i ^ 1)
    mid = to_near[BK:, :] + near[BK:, :]
    far = permute(jnp.concatenate([to_far, mid]), lambda i: i + 1 if i % 2 else i - 1)
    farther = permute(far[BK:, :], lambda i: i ^ 1)
    l3 = jnp.mean(mid.reshape(2, 16, WIDE).astype(F32), axis=1).astype(BF16)
    groups = [[2 * i + parity for i in range(blocks // 2)] for parity in range(2)]
    l3 = lax.all_to_all(
        jnp.broadcast_to(l3[None], (blocks // 2, 2, WIDE)), "seq", 0, 0, axis_index_groups=groups
    )
    l3 = jnp.swapaxes(l3, 0, 1)

    w_far_z = permute(w_far_y, lambda i: i ^ 16)
    w_cross_y = swap(w_far_y, 1)
    w_cross_z = swap(w_far_z, 1)

    outs = {}
    for bit in (2, 3, 1, 0):
        dest = h ^ bit
        info = jnp.stack([s, 2 * dest, 2 * dest + 1]).astype(jnp.int32)
        part = attend(total, info, queries, keys, values, l1, mid, near, far, farther, l3)
        outs[bit] = swap(part, bit) if bit else part

    return project(
        jnp.stack([half]).astype(jnp.int32),
        [outs[0], outs[1], outs[2], outs[3]],
        [out_weight, w_near, w_far_y, w_far_z, w_cross_y, w_cross_z],
    )


def solution(mesh):
    placed = (P("seq", "head"), P("seq", "head"), P("seq", "head"), P("head", None))
    return jax.shard_map(
        body, mesh=mesh, in_specs=placed, out_specs=P(("seq", "head"), None), check_vma=False
    )
```

time: 368 us -> 122 us (0.33)
  waiting for transfers between devices: 236 us -> 34.7 us
  Pallas kernels: 0 us -> 49.7 us
  other arithmetic: 37.7 us -> 0.34 us
  local copies, waits for them, and re-layouts: 44.1 us -> 8.49 us
  matrix products: 20.9 us -> 0 us
  starting transfers between devices: 11.2 us -> 28.7 us
  between operations: 13.6 us -> 0.12 us
  loops' own time: 3.97 us -> 0 us
    reduce_scatter x1 -> x0, waiting for transfers between devices: 151 us -> none  [body(): lax.psum_scatter(jnp.dot(attended, out_weight, preferred_element_type=jnp...]
    all_gather x1 -> x0, waiting for transfers between devices: 82.2 us -> none  [body(): middle = lax.all_gather(pooled(stack, 256), 'seq', axis=1, tiled=True)]
    pallas_call x0 -> x6, Pallas kernels: none -> 49.7 us  [the longest x4 39.9 us: attend(): pl.pallas_call(functools.partial(attend_kernel, total), grid_spec=pltpu.P...]
    ppermute x4 -> x11, waiting for transfers between devices: 2.77 us -> 24.8 us  [the longest x7 22.3 us: swap(): return lax.ppermute(array, 'head', [(i, i ^ bit) for i in range(4)])]
    dot_general x9 -> x0, matrix products: 20.9 us -> none  [the longest x1 9.75 us: body(): jnp.dot(attended, out_weight, preferred_element_type=jnp.float32)]
    concatenate x64 -> x0, local copies, waits for them, and re-layouts: 15.5 us -> none  [the longest x32 11.9 us: attend_block(): jnp.concatenate([fine_window[0], coarse_window[0], middle_window[0], summ...]
    ppermute x4 -> x11, starting transfers between devices: 11.1 us -> 24.9 us  [the longest x4 15.1 us: permute(): lax.ppermute(array, 'seq', [(i, move(i) % blocks) for i in range(blocks)])]
    sub x4 -> x0, other arithmetic: 13 us -> none  [attend_block(): expo = jnp.where(mask[None], jnp.exp(scores - peak), 0.0)]
  transfers between devices with their start and end apart: 6 -> 12, of which waited for: 3 -> 4; matrix products, arithmetic and copies ran while one was open for 2% -> 1% of each run, Pallas kernels for 0% -> 34%
where the time goes in v1:
time: 122 us
  Pallas kernels  49.7 us (41%)
  waiting for transfers between devices  34.7 us (28%)
  starting transfers between devices  28.7 us (24%)
  local copies, waits for them, and re-layouts  8.49 us (7%)
    pallas_call x4, Pallas kernels, attend(): pl.pallas_call(functools.partial(attend_kernel, total), grid_spec=pltpu.P...  39.9 us
    ppermute x7, waiting for transfers between devices, swap(): return lax.ppermute(array, 'head', [(i, i ^ bit) for i in range(4)])  22.3 us
    ppermute x4, starting transfers between devices, permute(): lax.ppermute(array, 'seq', [(i, move(i) % blocks) for i in range(blocks)])  15.1 us
    all_to_all x1, waiting for transfers between devices, body(): lax.all_to_all(jnp.broadcast_to(l3[None], (blocks // 2, 2, WIDE)), 'seq',...  9.93 us
    ppermute x7, starting transfers between devices, swap(): return lax.ppermute(array, 'head', [(i, i ^ bit) for i in range(4)])  9.74 us
    pallas_call x1, Pallas kernels, project(): pl.pallas_call(project_kernel, grid_spec=pltpu.PrefetchScalarGridSpec(num...  8.68 us
    unnamed x10, local copies, waits for them, and re-layouts  6.37 us
    all_to_all x1, starting transfers between devices, body(): lax.all_to_all(jnp.broadcast_to(l3[None], (blocks // 2, 2, WIDE)), 'seq',...  3.85 us
  transfers between devices with their start and end apart: 12, of which 4 were waited for; matrix products, arithmetic and copies ran while one was open for 1% of the time, Pallas kernels for 34%

profile of v1, /device:TPU:1, one launch (start us, length us, event | category | flops | bytes accessed | tf_op | source)
XLA Modules:
  0.0 122.1 jit_solution(5426240960982758137)
XLA Ops:
  0.0 1.4 %constant_dynamic-slice_fusion = bf16[256,2048]{1,0:T(8,128)(2,1)S(1)} fusion(bf16[512,2048]{1,0:T(8,128)(2,1)} %w0.1, s32[]{:T(128)S(6)} %select_n.16), kind=kLoop, calls=%fused_computation.9 | loop fusion | bytes 2097156 | tf_op jit(solution)/shard_map/dynamic_slice | solution.py:270
  1.4 2.2 %collective-permute-start.7 = (bf16[256,2048]{1,0:T(8,128)(2,1)S(1)}, bf16[256,2048]{1,0:T(8,128)(2,1)}, u32[]{:S(2)}, u32[]{:S(2)}) collective-permute-start(bf16[256,2048]{1,0:T(8,128)(2,1)S(1)} %constant_dynamic-slice_fusion), channel_id=1, source_target_pairs={{0,2},{1,3},{2,0},{3,1},{4,6},{5,7},{6,4},{7,5},{8,10},{9,11},{10,... | collective-permute-start | bytes 3145736 | tf_op jit(solution)/shard_map/ppermute | solution.py:268
  3.7 1.2 collective-permute-start.6
  4.9 20.4 %collective-permute-done.7.w2y = bf16[256,2048]{1,0:T(8,128)(2,1)} collective-permute-done((bf16[256,2048]{1,0:T(8,128)(2,1)S(1)}, bf16[256,2048]{1,0:T(8,128)(2,1)}, u32[]{:S(2)}, u32[]{:S(2)}) %collective-permute-start.7) | collective-permute-done | bytes 1048608 | tf_op jit(solution)/shard_map/ppermute | solution.py:268
  25.3 2.4 %collective-permute-start.8 = (bf16[256,2048]{1,0:T(8,128)(2,1)}, bf16[256,2048]{1,0:T(8,128)(2,1)}, u32[]{:S(2)}, u32[]{:S(2)}) collective-permute-start(bf16[256,2048]{1,0:T(8,128)(2,1)} %collective-permute-done.7.w2y), channel_id=1, source_target_pairs={{0,64},{4,68},{8,72},{12,76},{16,80},{20,84},{24,88},{28,92},{32,9... | collective-permute-start | bytes 3145736 | tf_op jit(solution)/shard_map/ppermute | solution.py:265
  27.7 1.6 %copy-done.1 = bf16[2048,512]{1,0:T(8,128)(2,1)S(1)} copy-done((bf16[2048,512]{1,0:T(8,128)(2,1)S(1)}, bf16[2048,512]{1,0:T(8,128)(2,1)}, u32[]{:S(2)}) %copy-start.1) | copy-done | bytes 2097176
  29.3 1.2 pool.1
  30.5 1.7 %collective-permute-start = (bf16[96,512]{1,0:T(8,128)(2,1)S(1)}, bf16[96,512]{1,0:T(8,128)(2,1)S(1)}, u32[]{:S(2)}, u32[]{:S(2)}) collective-permute-start(bf16[96,512]{1,0:T(8,128)(2,1)S(1)} %get-tuple-element.9), channel_id=1, source_target_pairs={{0,4},{4,0},{8,12},{12,8},{16,20},{20,16},{24,28},{28,24},{32,36},... | collective-permute-start | bytes 294920 | tf_op jit(solution)/shard_map/ppermute | solution.py:265
  32.2 2.4 %collective-permute-done.near_ref = bf16[96,512]{1,0:T(8,128)(2,1)S(1)} collective-permute-done((bf16[96,512]{1,0:T(8,128)(2,1)S(1)}, bf16[96,512]{1,0:T(8,128)(2,1)S(1)}, u32[]{:S(2)}, u32[]{:S(2)}) %collective-permute-start) | collective-permute-done | bytes 98336 | tf_op jit(solution)/shard_map/ppermute | solution.py:265
  34.7 9.6 %collective-permute-start.1 = (bf16[96,512]{1,0:T(8,128)(2,1)S(1)}, bf16[96,512]{1,0:T(8,128)(2,1)S(1)}, u32[]{:S(2)}, u32[]{:S(2)}) collective-permute-start(bf16[96,512]{1,0:T(8,128)(2,1)S(1)} %pad_maximum_fusion), channel_id=1, source_target_pairs={{0,252},{4,8},{8,4},{12,16},{16,12},{20,24},{24,20},{28,32},{32,28... | collective-permute-start | bytes 294920 | tf_op jit(solution)/shard_map/ppermute | solution.py:265
  44.3 0.7 broadcast_in_dim.2
  45.0 3.9 %all-to-all-start = ((bf16[32,2,512]{2,1,0:T(2,128)(2,1)}), bf16[32,2,512]{2,1,0:T(2,128)(2,1)S(1)}, u32[]{:S(2)}, u32[]{:S(2)}) async-start(bf16[32,2,512]{2,1,0:T(2,128)(2,1)} %broadcast_in_dim.2), calls=%async_computation | async-start | bytes 131072 | tf_op jit(solution)/shard_map/all_to_all | solution.py:280
  48.9 1.3 %collective-permute-start.2 = (bf16[32,512]{1,0:T(8,128)(2,1)S(1)}, bf16[32,512]{1,0:T(8,128)(2,1)S(1)}, u32[]{:S(2)}, u32[]{:S(2)}) collective-permute-start(bf16[32,512]{1,0:T(8,128)(2,1)S(1)} %slice.13), channel_id=1, source_target_pairs={{0,4},{4,0},{8,12},{12,8},{16,20},{20,16},{24,28},{28,24},{32,36},... | collective-permute-start | bytes 98312 | tf_op jit(solution)/shard_map/ppermute | solution.py:265
  50.2 0.1 pad_add_fusion.1.info
  50.3 9.9 %all-to-all-done = bf16[32,2,512]{2,1,0:T(2,128)(2,1)S(1)} async-done(((bf16[32,2,512]{2,1,0:T(2,128)(2,1)}), bf16[32,2,512]{2,1,0:T(2,128)(2,1)S(1)}, u32[]{:S(2)}, u32[]{:S(2)}) %all-to-all-start) | async-done | bytes 65568 | tf_op jit(solution)/shard_map/all_to_all | solution.py:280
  60.3 1.6 %copy-done.2 = bf16[2048,512]{1,0:T(8,128)(2,1)S(1)} copy-done((bf16[2048,512]{1,0:T(8,128)(2,1)S(1)}, bf16[2048,512]{1,0:T(8,128)(2,1)}, u32[]{:S(2)}) %copy-start.2) | copy-done | bytes 2097176
  61.8 9.7 %attend.5 = bf16[512,512]{1,0:T(8,128)(2,1)S(1)} custom-call(s32[3]{0:T(128)S(1)} %pad_add_fusion.1.info, bf16[2048,512]{1,0:T(8,128)(2,1)S(1)} %copy-done.2, bf16[2048,512]{1,0:T(8,128)(2,1)S(1)} %copy-done, bf16[2048,512]{1,0:T(8,128)(2,1)S(1)} %copy-done, bf16[2048,512]{1,0:T(8,128)(2,1)S(1)} %copy-done, bf16[2048,512]{1,0:T(8,128)(2,1)} %vn_ref.7, ...), custom_call_target="tpu_custom_call" | custom-call | flops 268435456 | bytes 2097152 | tf_op jit(solution)/shard_map/attend/pallas_call | solution.py:200
  71.5 4.1 %collective-permute-start.3 = (bf16[512,512]{1,0:T(8,128)(2,1)S(1)}, bf16[512,512]{1,0:T(8,128)(2,1)}, u32[]{:S(2)}, u32[]{:S(2)}) collective-permute-start(bf16[512,512]{1,0:T(8,128)(2,1)S(1)} %attend.5), channel_id=1, source_target_pairs={{0,1},{1,0},{2,3},{3,2},{4,5},{5,4},{6,7},{7,6},{8,9},{9,8},{10,11... | collective-permute-start | bytes 1572872 | tf_op jit(solution)/shard_map/ppermute | solution.py:268
  75.6 0.1 collective-permute-start.9
  75.7 0.4 collective-permute-start.10
  76.1 0.1 pad_add_fusion.2.info
  76.2 0.1 pad_add_fusion.3.info
  76.3 1.6 %copy-done.3 = bf16[2048,512]{1,0:T(8,128)(2,1)S(1)} copy-done((bf16[2048,512]{1,0:T(8,128)(2,1)S(1)}, bf16[2048,512]{1,0:T(8,128)(2,1)}, u32[]{:S(2)}) %copy-start.3) | copy-done | bytes 2097176
  77.9 10.3 %attend.6 = bf16[512,512]{1,0:T(8,128)(2,1)} custom-call(s32[3]{0:T(128)S(1)} %pad_add_fusion.2.info, bf16[2048,512]{1,0:T(8,128)(2,1)S(1)} %copy-done.3, bf16[2048,512]{1,0:T(8,128)(2,1)S(1)} %copy-done, bf16[2048,512]{1,0:T(8,128)(2,1)S(1)} %copy-done, bf16[2048,512]{1,0:T(8,128)(2,1)S(1)} %copy-done, bf16[2048,512]{1,0:T(8,128)(2,1)} %vn_ref.7, ...), custom_call_target="tpu_custom_call" | custom-call | flops 268435456 | bytes 2097152 | tf_op jit(solution)/shard_map/attend/pallas_call | solution.py:200
  88.1 0.4 collective-permute-start.4
  88.6 10.3 %attend.7 = bf16[512,512]{1,0:T(8,128)(2,1)} custom-call(s32[3]{0:T(128)S(1)} %pad_add_fusion.3.info, bf16[2048,512]{1,0:T(8,128)(2,1)S(1)} %copy-done.3, bf16[2048,512]{1,0:T(8,128)(2,1)S(1)} %copy-done, bf16[2048,512]{1,0:T(8,128)(2,1)S(1)} %copy-done, bf16[2048,512]{1,0:T(8,128)(2,1)S(1)} %copy-done, bf16[2048,512]{1,0:T(8,128)(2,1)} %vn_ref.7, ...), custom_call_target="tpu_custom_call" | custom-call | flops 268435456 | bytes 2097152 | tf_op jit(solution)/shard_map/attend/pallas_call | solution.py:200
  98.8 1.3 %collective-permute-start.5 = (bf16[512,512]{1,0:T(8,128)(2,1)}, bf16[512,512]{1,0:T(8,128)(2,1)S(1)}, u32[]{:S(2)}, u32[]{:S(2)}) collective-permute-start(bf16[512,512]{1,0:T(8,128)(2,1)} %attend.7), channel_id=1, source_target_pairs={{0,3},{1,2},{2,1},{3,0},{4,7},{5,6},{6,5},{7,4},{8,11},{9,10},{10,... | collective-permute-start | bytes 1572872 | tf_op jit(solution)/shard_map/ppermute | solution.py:268
  100.2 0.1 pad_add_fusion.info
  100.2 1.6 %copy-done.4 = bf16[2048,512]{1,0:T(8,128)(2,1)S(1)} copy-done((bf16[2048,512]{1,0:T(8,128)(2,1)S(1)}, bf16[2048,512]{1,0:T(8,128)(2,1)}, u32[]{:S(2)}) %copy-start.4) | copy-done | bytes 2097176
  101.8 9.6 %attend.4.a0 = bf16[512,512]{1,0:T(8,128)(2,1)S(1)} custom-call(s32[3]{0:T(128)S(1)} %pad_add_fusion.info, bf16[2048,512]{1,0:T(8,128)(2,1)S(1)} %copy-done.4, bf16[2048,512]{1,0:T(8,128)(2,1)S(1)} %copy-done, bf16[2048,512]{1,0:T(8,128)(2,1)S(1)} %copy-done, bf16[2048,512]{1,0:T(8,128)(2,1)S(1)} %copy-done, bf16[2048,512]{1,0:T(8,128)(2,1)} %vn_ref.7, ...), custom_call_target="tpu_custom_call" | custom-call | flops 268435456 | bytes 2097152 | tf_op jit(solution)/shard_map/attend/pallas_call | solution.py:200
  111.5 1.9 %collective-permute-done.5.a3 = bf16[512,512]{1,0:T(8,128)(2,1)S(1)} collective-permute-done((bf16[512,512]{1,0:T(8,128)(2,1)}, bf16[512,512]{1,0:T(8,128)(2,1)S(1)}, u32[]{:S(2)}, u32[]{:S(2)}) %collective-permute-start.5) | collective-permute-done | bytes 524320 | tf_op jit(solution)/shard_map/ppermute | solution.py:268
  113.4 8.7 %project.1 = bf16[512,2048]{1,0:T(8,128)(2,1)} custom-call(s32[1]{0:T(128)} %bitcast.info, bf16[512,512]{1,0:T(8,128)(2,1)S(1)} %attend.4.a0, bf16[512,512]{1,0:T(8,128)(2,1)} %collective-permute-done.3.a1, bf16[512,512]{1,0:T(8,128)(2,1)} %collective-permute-done.4.a2, bf16[512,512]{1,0:T(8,128)(2,1)S(1)} %collective-permute-done.5.a3, ...), custom_call_target="tpu_custom_call" | custom-call | flops 4294967296 | bytes 8388608 | tf_op jit(solution)/shard_map/project/pallas_call | solution.py:239
  (19 shorter events, 0.1 us)
Async XLA Ops:
  0.0 27.7 %copy-start = (bf16[2048,512]{1,0:T(8,128)(2,1)S(1)}, bf16[2048,512]{1,0:T(8,128)(2,1)}, u32[]{:S(2)}) copy-start(bf16[2048,512]{1,0:T(8,128)(2,1)} %kn_ref.7) | copy-start | bytes 6291460
  1.4 23.8 %collective-permute-start.7 = (bf16[256,2048]{1,0:T(8,128)(2,1)S(1)}, bf16[256,2048]{1,0:T(8,128)(2,1)}, u32[]{:S(2)}, u32[]{:S(2)}) collective-permute-start(bf16[256,2048]{1,0:T(8,128)(2,1)S(1)} %constant_dynamic-slice_fusion), channel_id=1, source_target_pairs={{0,2},{1,3},{2,0},{3,1},{4,6},{5,7},{6,4},{7,5},{8,10},{9,11},{10,... | collective-permute-start | bytes 3145736 | tf_op jit(solution)/shard_map/ppermute | solution.py:268
  3.7 109.7 %collective-permute-start.6 = (bf16[512,2048]{1,0:T(8,128)(2,1)}, bf16[512,2048]{1,0:T(8,128)(2,1)}, u32[]{:S(2)}, u32[]{:S(2)}) collective-permute-start(bf16[512,2048]{1,0:T(8,128)(2,1)} %w0.1), channel_id=1, source_target_pairs={{0,1},{1,0},{2,3},{3,2},{4,5},{5,4},{6,7},{7,6},{8,9},{9,8},{10,11... | collective-permute-start | bytes 6291464 | tf_op jit(solution)/shard_map/ppermute | solution.py:268
  25.3 50.4 %collective-permute-start.8 = (bf16[256,2048]{1,0:T(8,128)(2,1)}, bf16[256,2048]{1,0:T(8,128)(2,1)}, u32[]{:S(2)}, u32[]{:S(2)}) collective-permute-start(bf16[256,2048]{1,0:T(8,128)(2,1)} %collective-permute-done.7.w2y), channel_id=1, source_target_pairs={{0,64},{4,68},{8,72},{12,76},{16,80},{20,84},{24,88},{28,92},{32,9... | collective-permute-start | bytes 3145736 | tf_op jit(solution)/shard_map/ppermute | solution.py:265
  27.7 1.6 %copy-start.1 = (bf16[2048,512]{1,0:T(8,128)(2,1)S(1)}, bf16[2048,512]{1,0:T(8,128)(2,1)}, u32[]{:S(2)}) copy-start(bf16[2048,512]{1,0:T(8,128)(2,1)} %vn_ref.7) | copy-start | bytes 6291460
  30.5 4.1 %collective-permute-start = (bf16[96,512]{1,0:T(8,128)(2,1)S(1)}, bf16[96,512]{1,0:T(8,128)(2,1)S(1)}, u32[]{:S(2)}, u32[]{:S(2)}) collective-permute-start(bf16[96,512]{1,0:T(8,128)(2,1)S(1)} %get-tuple-element.9), channel_id=1, source_target_pairs={{0,4},{4,0},{8,12},{12,8},{16,20},{20,16},{24,28},{28,24},{32,36},... | collective-permute-start | bytes 294920 | tf_op jit(solution)/shard_map/ppermute | solution.py:265
  34.7 14.2 %collective-permute-start.1 = (bf16[96,512]{1,0:T(8,128)(2,1)S(1)}, bf16[96,512]{1,0:T(8,128)(2,1)S(1)}, u32[]{:S(2)}, u32[]{:S(2)}) collective-permute-start(bf16[96,512]{1,0:T(8,128)(2,1)S(1)} %pad_maximum_fusion), channel_id=1, source_target_pairs={{0,252},{4,8},{8,4},{12,16},{16,12},{20,24},{24,20},{28,32},{32,28... | collective-permute-start | bytes 294920 | tf_op jit(solution)/shard_map/ppermute | solution.py:265
  45.0 15.2 %all-to-all-start = ((bf16[32,2,512]{2,1,0:T(2,128)(2,1)}), bf16[32,2,512]{2,1,0:T(2,128)(2,1)S(1)}, u32[]{:S(2)}, u32[]{:S(2)}) async-start(bf16[32,2,512]{2,1,0:T(2,128)(2,1)} %broadcast_in_dim.2), calls=%async_computation | async-start | bytes 131072 | tf_op jit(solution)/shard_map/all_to_all | solution.py:280
  48.9 11.4 %collective-permute-start.2 = (bf16[32,512]{1,0:T(8,128)(2,1)S(1)}, bf16[32,512]{1,0:T(8,128)(2,1)S(1)}, u32[]{:S(2)}, u32[]{:S(2)}) collective-permute-start(bf16[32,512]{1,0:T(8,128)(2,1)S(1)} %slice.13), channel_id=1, source_target_pairs={{0,4},{4,0},{8,12},{12,8},{16,20},{20,16},{24,28},{28,24},{32,36},... | collective-permute-start | bytes 98312 | tf_op jit(solution)/shard_map/ppermute | solution.py:265
  60.2 1.6 %copy-start.2 = (bf16[2048,512]{1,0:T(8,128)(2,1)S(1)}, bf16[2048,512]{1,0:T(8,128)(2,1)}, u32[]{:S(2)}) copy-start(bf16[2048,512]{1,0:T(8,128)(2,1)} %q_ref.7) | copy-start | bytes 6291460
  71.5 27.3 %collective-permute-start.3 = (bf16[512,512]{1,0:T(8,128)(2,1)S(1)}, bf16[512,512]{1,0:T(8,128)(2,1)}, u32[]{:S(2)}, u32[]{:S(2)}) collective-permute-start(bf16[512,512]{1,0:T(8,128)(2,1)S(1)} %attend.5), channel_id=1, source_target_pairs={{0,1},{1,0},{2,3},{3,2},{4,5},{5,4},{6,7},{7,6},{8,9},{9,8},{10,11... | collective-permute-start | bytes 1572872 | tf_op jit(solution)/shard_map/ppermute | solution.py:268
  75.6 37.8 %collective-permute-start.9 = (bf16[256,2048]{1,0:T(8,128)(2,1)}, bf16[256,2048]{1,0:T(8,128)(2,1)}, u32[]{:S(2)}, u32[]{:S(2)}) collective-permute-start(bf16[256,2048]{1,0:T(8,128)(2,1)} %collective-permute-done.7.w2y), channel_id=1, source_target_pairs={{0,1},{1,0},{2,3},{3,2},{4,5},{5,4},{6,7},{7,6},{8,9},{9,8},{10,11... | collective-permute-start | bytes 3145736 | tf_op jit(solution)/shard_map/ppermute | solution.py:268
  75.7 37.7 %collective-permute-start.10 = (bf16[256,2048]{1,0:T(8,128)(2,1)}, bf16[256,2048]{1,0:T(8,128)(2,1)}, u32[]{:S(2)}, u32[]{:S(2)}) collective-permute-start(bf16[256,2048]{1,0:T(8,128)(2,1)} %collective-permute-done.8.w2z), channel_id=1, source_target_pairs={{0,1},{1,0},{2,3},{3,2},{4,5},{5,4},{6,7},{7,6},{8,9},{9,8},{10,11... | collective-permute-start | bytes 3145736 | tf_op jit(solution)/shard_map/ppermute | solution.py:268
  76.3 1.6 %copy-start.3 = (bf16[2048,512]{1,0:T(8,128)(2,1)S(1)}, bf16[2048,512]{1,0:T(8,128)(2,1)}, u32[]{:S(2)}) copy-start(bf16[2048,512]{1,0:T(8,128)(2,1)} %q_ref.7) | copy-start | bytes 6291460
  88.1 23.3 %collective-permute-start.4 = (bf16[512,512]{1,0:T(8,128)(2,1)}, bf16[512,512]{1,0:T(8,128)(2,1)}, u32[]{:S(2)}, u32[]{:S(2)}) collective-permute-start(bf16[512,512]{1,0:T(8,128)(2,1)} %attend.6), channel_id=1, source_target_pairs={{0,2},{1,3},{2,0},{3,1},{4,6},{5,7},{6,4},{7,5},{8,10},{9,11},{10,... | collective-permute-start | bytes 1572872 | tf_op jit(solution)/shard_map/ppermute | solution.py:268
  98.8 14.5 %collective-permute-start.5 = (bf16[512,512]{1,0:T(8,128)(2,1)}, bf16[512,512]{1,0:T(8,128)(2,1)S(1)}, u32[]{:S(2)}, u32[]{:S(2)}) collective-permute-start(bf16[512,512]{1,0:T(8,128)(2,1)} %attend.7), channel_id=1, source_target_pairs={{0,3},{1,2},{2,1},{3,0},{4,7},{5,6},{6,5},{7,4},{8,11},{9,10},{10,... | collective-permute-start | bytes 1572872 | tf_op jit(solution)/shard_map/ppermute | solution.py:268
  100.2 1.6 %copy-start.4 = (bf16[2048,512]{1,0:T(8,128)(2,1)S(1)}, bf16[2048,512]{1,0:T(8,128)(2,1)}, u32[]{:S(2)}) copy-start(bf16[2048,512]{1,0:T(8,128)(2,1)} %q_ref.7) | copy-start | bytes 6291460

commit v2 on v1

v2 whole, which is shorter than its diff:
```python
import functools

import jax
import jax.numpy as jnp
from jax import lax
from jax.experimental import pallas as pl
from jax.experimental.pallas import tpu as pltpu
from jax.sharding import PartitionSpec as P

HD = 128
HEADS = 4
WIDE = HEADS * HD
LOG2E = 1.4426950408889634
SCORE = HD**-0.5 * LOG2E
NEG = -1e30
F32 = jnp.float32
BF16 = jnp.bfloat16
POOL_VMEM, ATTEND_VMEM, PROJECT_VMEM = (mib * 1024 * 1024 for mib in (51, 51, 24))
CHUNKS = 4
ORDER = ((0, 2), (1, 1), (2, 3), (3, 0))
SMALL = pl.CostEstimate(flops=1000, bytes_accessed=1000, transcendentals=0)

TK, TV, AK, AV, BK, BV = (16 * i for i in range(6))


def mean_rows(count, size, scale):
    rows = lax.broadcasted_iota(jnp.int32, (count, count * size), 0)
    cols = lax.broadcasted_iota(jnp.int32, (count, count * size), 1)
    return jnp.where(rows == cols // size, scale, 0.0).astype(BF16)


def pool_kernel(k_hbm, v_hbm, l1_ref, near_ref, far_ref, k_ref, v_ref, sems):
    odd = lax.axis_index("seq") % 2
    ones = mean_rows(16, 16, 1.0)
    chunk = k_ref.shape[0] // CHUNKS
    copies = []
    for i in range(CHUNKS):
        rows = pl.ds(chunk * i, chunk)
        for which, (hbm, ref) in enumerate(((k_hbm, k_ref), (v_hbm, v_ref))):
            copy = pltpu.make_async_copy(hbm.at[rows, :], ref.at[rows, :], sems.at[which, i])
            copy.start()
            copies.append(copy)
    level2 = [[], []]
    for i in range(CHUNKS):
        for which, ref in enumerate((k_ref, v_ref)):
            copies[2 * i + which].wait()
            for at in range(chunk * i, chunk * (i + 1), 256):
                total = jnp.dot(ones, ref[at : at + 256, :], preferred_element_type=F32)
                l1_ref[which, at // 16 : at // 16 + 16, :] = (total * 0.0625).astype(BF16)
                level2[which].append(jnp.sum(total, axis=0, keepdims=True) * (1.0 / 256.0))

    last = k_ref.shape[0]
    low = [k_ref[0:16, :], v_ref[0:16, :], l1_ref[0, 0:16, :], l1_ref[1, 0:16, :]]
    high = [k_ref[last - 16 : last, :], v_ref[last - 16 : last, :]]
    high += [l1_ref[which, last // 16 - 16 : last // 16, :] for which in range(2)]
    for at, (below, above) in enumerate(zip(low, high)):
        rows = slice(16 * at, 16 * at + 16)
        near_ref[rows, :] = jnp.where(odd == 1, below, above)
        far_ref[rows, :] = jnp.where(odd == 1, above, below)
    row = lax.broadcasted_iota(jnp.int32, (16, WIDE), 0)
    for which, at in ((0, BK), (1, BV)):
        both = jnp.concatenate(level2[which] * 2, axis=0)
        near_ref[at : at + 16, :] = jnp.where(row // 8 == odd, both, 0.0).astype(BF16)


def pool(keys, values):
    rows = keys.shape[0]
    return pl.pallas_call(
        pool_kernel,
        in_specs=[
            pl.BlockSpec(memory_space=pltpu.HBM),
            pl.BlockSpec(memory_space=pltpu.HBM),
        ],
        out_specs=[pl.BlockSpec(memory_space=pltpu.VMEM)] * 3,
        scratch_shapes=[
            pltpu.VMEM((rows, WIDE), BF16),
            pltpu.VMEM((rows, WIDE), BF16),
            pltpu.SemaphoreType.DMA((2, CHUNKS)),
        ],
        out_shape=[
            jax.ShapeDtypeStruct((2, rows // 16, WIDE), BF16),
            jax.ShapeDtypeStruct((96, WIDE), BF16),
            jax.ShapeDtypeStruct((64, WIDE), BF16),
        ],
        cost_estimate=pl.CostEstimate(flops=4000000000, bytes_accessed=14000000, transcendentals=0),
        compiler_params=pltpu.CompilerParams(vmem_limit_bytes=POOL_VMEM),
        name="pool",
    )(keys, values)


def middle_kernel(own_ref, near_ref, far_ref, to_far_ref, l3_ref):
    to_far_ref[0:64, :] = far_ref[...]
    means = []
    for at in (BK, BV):
        rows = slice(at, at + 16)
        pair = own_ref[rows, :].astype(F32) + near_ref[rows, :].astype(F32)
        to_far_ref[rows, :] = pair.astype(BF16)
        means.append(jnp.sum(pair, axis=0, keepdims=True) * 0.0625)
    both = jnp.concatenate(means, axis=0).astype(BF16)
    l3_ref[...] = jnp.broadcast_to(both[None], l3_ref.shape)


def middle(own, near, far, copies):
    return pl.pallas_call(
        middle_kernel,
        out_shape=[
            jax.ShapeDtypeStruct((96, WIDE), BF16),
            jax.ShapeDtypeStruct((copies, 2, WIDE), BF16),
        ],
        cost_estimate=pl.CostEstimate(flops=1000000000, bytes_accessed=3500000, transcendentals=0),
        compiler_params=pltpu.CompilerParams(vmem_limit_bytes=4 * 1024 * 1024),
        name="middle",
    )(own, near, far)


def attend_kernel(
    total, base, info, q_ref, k_ref, kp_ref, kn_ref, v_ref, vp_ref, vn_ref, l1_ref, mid_ref, near_ref,
    far_ref, farther_ref, l3_ref, out_ref, kx, vx, l1x, sk, sv,
):
    step = pl.program_id(0)
    block = info[0]
    group = info[1 + base + step]
    odd = block % 2
    last_group = 2048 // 256 - 1

    @pl.when(step == 0)
    def _():
        for which, at in ((0, AK), (1, AV)):
            near, far = near_ref[at : at + 16, :], far_ref[at : at + 16, :]
            l1x[which, 0:16, :] = jnp.where(odd == 1, near, far)
            l1x[which, 16:144, :] = l1_ref[which]
            l1x[which, 144:160, :] = jnp.where(odd == 1, far, near)
        for scratch, at, which in ((sk, BK, 0), (sv, BV, 1)):
            scratch[48:64, :] = mid_ref[at : at + 16, :]
            scratch[64:80, :] = far_ref[at : at + 16, :]
            scratch[80:96, :] = farther_ref[at - BK : at - BK + 16, :]
            here = lax.broadcasted_iota(jnp.int32, (32, 2, WIDE), 1) == which
            picked = jnp.sum(jnp.where(here, l3_ref[...].astype(F32), 0.0), axis=1)
            scratch[96:128, :] = picked.astype(BF16)
        zeros = jnp.zeros((32, WIDE), BF16)
        kx[288:320, :] = zeros
        vx[288:320, :] = zeros

    for scratch, main, before, after, at in (
        (kx, k_ref, kp_ref, kn_ref, TK),
        (vx, v_ref, vp_ref, vn_ref, TV),
    ):
        near, far = near_ref[at : at + 16, :], far_ref[at : at + 16, :]
        low = jnp.where(odd == 1, near, far)
        high = jnp.where(odd == 1, far, near)
        scratch[0:16, :] = jnp.where(group == 0, low, before[...])
        scratch[16:272, :] = main[...]
        scratch[272:288, :] = jnp.where(group == last_group, high, after[...])
    window = pl.ds(pl.multiple_of(16 * group, 16), 48)
    sk[0:48, :] = l1x[0, window, :]
    sv[0:48, :] = l1x[1, window, :]

    c = 8 * block + group
    e = block // 2
    col = lax.broadcasted_iota(jnp.int32, (64, 128), 1)
    fine = lax.broadcasted_iota(jnp.int32, (64, 128), 0) // 16
    tile = col // 16
    beside = jnp.where(odd == 0, e - 1, e + 1)
    across = jnp.where(odd == 0, e + 1, e - 1)
    m = 16 * jnp.where(tile == 3, e, jnp.where(tile == 4, beside, across)) + col % 16
    term2 = jnp.where((m >= 0) & (m < total // 256) & (jnp.abs(m - c) > 1), 0.0, NEG)
    term3 = jnp.where(jnp.abs(col - 96 - e) > 1, 0.0, NEG)
    j = 16 * (c - 1) + col
    term1 = jnp.where((j >= 0) & (j < total // 16), 0.0, NEG)
    shared = jnp.where(col < 48, term1, jnp.where(col < 96, term2, term3))

    pairs = [(part, head) for part in range(4) for head in range(HEADS)]
    cols = [slice(HD * head, HD * head + HD) for head in range(HEADS)]
    rows = [slice(64 * part, 64 * part + 64) for part in range(4)]
    near_rows = [slice(64 * part, 64 * part + 128) for part in range(4)]
    biases = []
    for part in range(4):
        token = 256 * c + 64 * part - 16 + col
        ok = (jnp.abs(tile - 1 - fine) <= 1) & (token >= 0) & (token < total)
        own = (col < 48) & (jnp.abs(col - 16 - 4 * part - fine) <= 1)
        terms = [jnp.where(ok, 0.0, NEG), jnp.where(own, NEG, shared)]
        biases.append(jnp.concatenate(terms, axis=1).astype(F32))
    scores, weights, sums = [], [], []
    for part, head in pairs:
        key_rows = jnp.concatenate([kx[near_rows[part], cols[head]], sk[:, cols[head]]], axis=0)
        raw = lax.dot_general(
            q_ref[rows[part], cols[head]], key_rows, (((1,), (1,)), ((), ())), preferred_element_type=F32
        )
        scores.append(raw * SCORE + biases[part])
    peaks = [jnp.max(score, axis=1, keepdims=True) for score in scores]
    for score, peak in zip(scores, peaks):
        expo = jnp.exp2(score - peak)
        sums.append(jnp.sum(expo, axis=1, keepdims=True))
        weights.append(expo.astype(BF16))
    summed = []
    for (part, head), weight in zip(pairs, weights):
        value_rows = jnp.concatenate([vx[near_rows[part], cols[head]], sv[:, cols[head]]], axis=0)
        summed.append(jnp.dot(weight, value_rows, preferred_element_type=F32))
    for (part, head), value, sum_ in zip(pairs, summed, sums):
        out_ref[rows[part], cols[head]] = (value * (1.0 / sum_)).astype(BF16)


def attend(total, base, info, queries, keys, values, l1, mid, near, far, farther, l3):
    def main(i, s):
        return (s[1 + base + i], 0)

    def before(i, s):
        return (jnp.maximum(16 * s[1 + base + i] - 1, 0), 0)

    def after(i, s):
        return (jnp.minimum(16 * s[1 + base + i] + 16, 127), 0)

    def whole(array):
        return pl.BlockSpec(array.shape, lambda i, s: (0,) * array.ndim)

    wide, thin_low, thin_high = (
        pl.BlockSpec((256, WIDE), main),
        pl.BlockSpec((16, WIDE), before),
        pl.BlockSpec((16, WIDE), after),
    )
    small = (l1, mid, near, far, farther, l3)
    return pl.pallas_call(
        functools.partial(attend_kernel, total, base),
        grid_spec=pltpu.PrefetchScalarGridSpec(
            num_scalar_prefetch=1,
            grid=(2,),
            in_specs=[wide, wide, thin_low, thin_high, wide, thin_low, thin_high]
            + [whole(array) for array in small],
            out_specs=pl.BlockSpec((256, WIDE), lambda i, s: (i, 0)),
            scratch_shapes=[
                pltpu.VMEM((320, WIDE), BF16),
                pltpu.VMEM((320, WIDE), BF16),
                pltpu.VMEM((2, 160, WIDE), BF16),
                pltpu.VMEM((128, WIDE), BF16),
                pltpu.VMEM((128, WIDE), BF16),
            ],
        ),
        out_shape=jax.ShapeDtypeStruct((512, WIDE), BF16),
        cost_estimate=pl.CostEstimate(flops=20000000000, bytes_accessed=70000000, transcendentals=0),
        compiler_params=pltpu.CompilerParams(vmem_limit_bytes=ATTEND_VMEM),
        name="attend",
    )(info, queries, keys, keys, keys, values, values, values, *small)


def project_kernel(n, m, *refs):
    weights, attended, before, out_ref = refs[:m], refs[m : n + m], refs[n + m : -1], refs[-1]
    left = jnp.concatenate([a[...] for a in attended], axis=1)
    right = jnp.concatenate([w[...] for w in weights], axis=0)
    total = jnp.dot(left, right, preferred_element_type=F32)
    if before:
        total += before[0][...]
    out_ref[...] = total.astype(out_ref.dtype)


def project(attended, weights, before, dtype):
    rows, columns = attended[0].shape[0], weights[0].shape[1]
    tile = 1024
    depth = WIDE * len(attended)

    def tiles(arrays):
        return [pl.BlockSpec((w.shape[0], tile), lambda i: (0, i)) for w in arrays]

    return pl.pallas_call(
        functools.partial(project_kernel, len(attended), len(weights)),
        grid=(columns // tile,),
        in_specs=[
            *tiles(weights),
            *(pl.BlockSpec(a.shape, lambda i: (0, 0)) for a in attended),
            *tiles(before),
        ],
        out_specs=pl.BlockSpec((rows, tile), lambda i: (0, i)),
        out_shape=jax.ShapeDtypeStruct((rows, columns), dtype),
        cost_estimate=pl.CostEstimate(flops=20000000000, bytes_accessed=70000000, transcendentals=0),
        compiler_params=pltpu.CompilerParams(vmem_limit_bytes=PROJECT_VMEM),
        name="project",
    )(*weights, *attended, *before)


def body(queries, keys, values, out_weight):
    blocks = lax.axis_size("seq")
    total = queries.shape[0] * blocks
    s = lax.axis_index("seq")
    h = lax.axis_index("head")

    def permute(array, move):
        return lax.ppermute(array, "seq", [(i, move(i) % blocks) for i in range(blocks)])

    def swap(array, bit):
        return lax.ppermute(array, "head", [(i, i ^ bit) for i in range(4)])

    def cross(array):
        pairs = []
        for i in range(blocks):
            for j in range(4):
                pairs.append((4 * i + j, 4 * (i ^ 8 if j % 2 else i) + (j ^ 2)))
        return lax.ppermute(array, ("seq", "head"), pairs)

    order = (2, 1, 3, 0)
    groups = [2 * (h ^ bit) + part for bit in order for part in range(2)]
    info = jnp.stack([s, *groups]).astype(jnp.int32)

    w_far = cross(out_weight)
    w_near = swap(out_weight, 1)
    l1, to_near, to_far = pool(keys, values)
    near = permute(to_near, lambda i: i ^ 1)
    to_far, l3 = middle(to_near, near, to_far, blocks // 2)
    far = permute(to_far, lambda i: i + 1 if i % 2 else i - 1)
    farther = permute(far[BK:, :], lambda i: i ^ 1)
    peers = [[2 * i + parity for i in range(blocks // 2)] for parity in range(2)]
    l3 = lax.all_to_all(l3, "seq", 0, 0, axis_index_groups=peers)

    w_far, far = lax.optimization_barrier((w_far, far))
    w_cross = swap(w_far, 1)
    outs = {}
    for at, bit in ORDER:
        part = attend(total, 2 * at, info, queries, keys, values, l1, to_far, near, far, farther, l3)
        outs[bit] = swap(part, bit) if bit else part

    inner = project([outs[0], outs[2], outs[1]], [out_weight, w_far, w_near], [], F32)
    return project([outs[3]], [w_cross], [inner], BF16)


def solution(mesh):
    placed = (P("seq", "head"), P("seq", "head"), P("seq", "head"), P("head", None))
    return jax.shard_map(
        body, mesh=mesh, in_specs=placed, out_specs=P(("seq", "head"), None), check_vma=False
    )
```

time: 122 us -> 69.2 us (0.57)
  Pallas kernels: 49.7 us -> 27.4 us
  waiting for transfers between devices: 34.7 us -> 14.8 us
  local copies, waits for them, and re-layouts: 8.49 us -> 1.69 us
  starting transfers between devices: 28.7 us -> 24.8 us
    pallas_call x6 -> x8, Pallas kernels: 49.7 us -> 27.4 us  [the longest x4 15.9 us: attend(): pl.pallas_call(functools.partial(attend_kernel, total, base), grid_spec=p...]
    ppermute x7 -> x5, waiting for transfers between devices: 22.3 us -> 2.79 us  [swap(): return lax.ppermute(array, 'head', [(i, i ^ bit) for i in range(4)])]
    ppermute x4 -> x3, starting transfers between devices: 15.1 us -> 8.58 us  [permute(): lax.ppermute(array, 'seq', [(i, move(i) % blocks) for i in range(blocks)])]
    unnamed x10 -> x4, local copies, waits for them, and re-layouts: 6.37 us -> 1.6 us
    ppermute x0 -> x1, starting transfers between devices: none -> 3.56 us  [cross(): return lax.ppermute(array, ('seq', 'head'), pairs)]
    ppermute x7 -> x5, starting transfers between devices: 9.74 us -> 7.08 us  [swap(): return lax.ppermute(array, 'head', [(i, i ^ bit) for i in range(4)])]
    all_to_all x1, waiting for transfers between devices: 9.93 us -> 7.68 us  [body(): l3 = lax.all_to_all(l3, 'seq', 0, 0, axis_index_groups=peers)]
    all_to_all x1, starting transfers between devices: 3.85 us -> 5.58 us  [body(): l3 = lax.all_to_all(l3, 'seq', 0, 0, axis_index_groups=peers)]
  transfers between devices with their start and end apart: 12 -> 10, of which waited for: 4 -> 4; matrix products, arithmetic and copies ran while one was open for 1% -> 0% of each run, Pallas kernels for 34% -> 36%
where the time goes in v2:
time: 69.2 us; the launch traced here: 68.9 us
  Pallas kernels  27.4 us (40%)
  starting transfers between devices  24.8 us (36%)
  waiting for transfers between devices  14.8 us (21%)
  local copies, waits for them, and re-layouts  1.69 us (2%)
    pallas_call x4, Pallas kernels, attend(): pl.pallas_call(functools.partial(attend_kernel, total, base), grid_spec=p...  15.9 us
    ppermute x3, starting transfers between devices, permute(): lax.ppermute(array, 'seq', [(i, move(i) % blocks) for i in range(blocks)])  8.58 us
    pallas_call x2, Pallas kernels, project(): pl.pallas_call(functools.partial(project_kernel, len(attended), len(weigh...  8.39 us
    all_to_all x1, waiting for transfers between devices, body(): l3 = lax.all_to_all(l3, 'seq', 0, 0, axis_index_groups=peers)  7.68 us
    ppermute x5, starting transfers between devices, swap(): return lax.ppermute(array, 'head', [(i, i ^ bit) for i in range(4)])  7.08 us
    all_to_all x1, starting transfers between devices, body(): l3 = lax.all_to_all(l3, 'seq', 0, 0, axis_index_groups=peers)  5.58 us
    ppermute x1, starting transfers between devices, cross(): return lax.ppermute(array, ('seq', 'head'), pairs)  3.56 us
    ppermute x3, waiting for transfers between devices, permute(): lax.ppermute(array, 'seq', [(i, move(i) % blocks) for i in range(blocks)])  3.43 us
  transfers between devices with their start and end apart: 10, of which 4 were waited for; matrix products, arithmetic and copies ran while one was open for 0% of the time, Pallas kernels for 36%

profile of v2, /device:TPU:1, one launch (start us, length us, event | category | flops | bytes accessed | tf_op | source)
XLA Modules:
  0.0 68.9 jit_solution(9439135416654337468)
XLA Ops:
  0.0 3.6 %collective-permute-start = (bf16[512,2048]{1,0:T(8,128)(2,1)}, bf16[512,2048]{1,0:T(8,128)(2,1)}, u32[]{:S(2)}, u32[]{:S(2)}) collective-permute-start(bf16[512,2048]{1,0:T(8,128)(2,1)} %refs_0_.1), channel_id=1, source_target_pairs={{0,2},{1,35},{2,0},{3,33},{4,6},{5,39},{6,4},{7,37},{8,10},{9,43},... | collective-permute-start | bytes 6291464 | tf_op jit(solution)/shard_map/ppermute | solution.py:296
  3.6 1.6 %copy-done = bf16[2048,512]{1,0:T(8,128)(2,1)S(1)} copy-done((bf16[2048,512]{1,0:T(8,128)(2,1)S(1)}, bf16[2048,512]{1,0:T(8,128)(2,1)}, u32[]{:S(2)}) %copy-start) | copy-done | bytes 2097176
  5.2 2.5 %pool.1 = (bf16[2,128,512]{2,1,0:T(8,128)(2,1)S(1)}, bf16[96,512]{1,0:T(8,128)(2,1)S(1)}, bf16[64,512]{1,0:T(8,128)(2,1)S(1)}) custom-call(bf16[2048,512]{1,0:T(8,128)(2,1)S(1)} %copy-done, bf16[2048,512]{1,0:T(8,128)(2,1)} %vn_ref.7), custom_call_target="tpu_custom_call" | custom-call | flops 4000000000 | bytes 14000000 | tf_op jit(solution)/shard_map/pool/pallas_call | solution.py:68
  7.7 0.0 copy-start.1
  7.7 1.7 %collective-permute-start.1 = (bf16[96,512]{1,0:T(8,128)(2,1)S(1)}, bf16[96,512]{1,0:T(8,128)(2,1)S(1)}, u32[]{:S(2)}, u32[]{:S(2)}) collective-permute-start(bf16[96,512]{1,0:T(8,128)(2,1)S(1)} %get-tuple-element.12.own_ref), channel_id=1, source_target_pairs={{0,4},{4,0},{8,12},{12,8},{16,20},{20,16},{24,28},{28,24},{32,36},... | collective-permute-start | bytes 294920 | tf_op jit(solution)/shard_map/ppermute | solution.py:286
  9.4 3.4 %collective-permute-done.1.near_ref = bf16[96,512]{1,0:T(8,128)(2,1)S(1)} collective-permute-done((bf16[96,512]{1,0:T(8,128)(2,1)S(1)}, bf16[96,512]{1,0:T(8,128)(2,1)S(1)}, u32[]{:S(2)}, u32[]{:S(2)}) %collective-permute-start.1) | collective-permute-done | bytes 98336 | tf_op jit(solution)/shard_map/ppermute | solution.py:286
  12.8 0.7 middle.1
  13.5 6.6 %collective-permute-start.2 = (bf16[96,512]{1,0:T(8,128)(2,1)S(1)}, bf16[96,512]{1,0:T(8,128)(2,1)S(1)}, u32[]{:S(2)}, u32[]{:S(2)}) collective-permute-start(bf16[96,512]{1,0:T(8,128)(2,1)S(1)} %get-tuple-element.14.mid_ref), channel_id=1, source_target_pairs={{0,252},{4,8},{8,4},{12,16},{16,12},{20,24},{24,20},{28,32},{32,28... | collective-permute-start | bytes 294920 | tf_op jit(solution)/shard_map/ppermute | solution.py:286
  20.1 5.6 %all-to-all-start = ((bf16[32,2,512]{2,1,0:T(2,128)(2,1)}), bf16[32,2,512]{2,1,0:T(2,128)(2,1)S(1)}, u32[]{:S(2)}, u32[]{:S(2)}) async-start(bf16[32,2,512]{2,1,0:T(2,128)(2,1)} %get-tuple-element.18), calls=%async_computation | async-start | bytes 131072 | tf_op jit(solution)/shard_map/all_to_all | solution.py:310
  25.7 0.0 collective-permute-done.2.far_ref
  25.7 0.2 collective-permute-start.4
  26.0 0.0 copy-done.1
  26.0 2.4 %collective-permute-start.6 = (bf16[512,2048]{1,0:T(8,128)(2,1)S(1)}, bf16[512,2048]{1,0:T(8,128)(2,1)}, u32[]{:S(2)}, u32[]{:S(2)}) collective-permute-start(bf16[512,2048]{1,0:T(8,128)(2,1)S(1)} %copy-done.1), channel_id=1, source_target_pairs={{0,1},{1,0},{2,3},{3,2},{4,5},{5,4},{6,7},{7,6},{8,9},{9,8},{10,11... | collective-permute-start | bytes 6291464 | tf_op jit(solution)/shard_map/ppermute | solution.py:289
  28.4 0.1 stack.39.info
  28.5 0.9 %collective-permute-done.refs_1_ = bf16[512,2048]{1,0:T(8,128)(2,1)} collective-permute-done((bf16[512,2048]{1,0:T(8,128)(2,1)}, bf16[512,2048]{1,0:T(8,128)(2,1)}, u32[]{:S(2)}, u32[]{:S(2)}) %collective-permute-start) | collective-permute-done | bytes 2097184 | tf_op jit(solution)/shard_map/ppermute | solution.py:296
  29.4 7.7 %all-to-all-done.l3_ref = bf16[32,2,512]{2,1,0:T(2,128)(2,1)S(1)} async-done(((bf16[32,2,512]{2,1,0:T(2,128)(2,1)}), bf16[32,2,512]{2,1,0:T(2,128)(2,1)S(1)}, u32[]{:S(2)}, u32[]{:S(2)}) %all-to-all-start) | async-done | bytes 65568 | tf_op jit(solution)/shard_map/all_to_all | solution.py:310
  37.1 0.0 collective-permute-done.4.farther_ref
  37.1 4.0 %attend.6 = bf16[512,512]{1,0:T(8,128)(2,1)S(1)} custom-call(s32[9]{0:T(128)S(1)} %stack.39.info, bf16[2048,512]{1,0:T(8,128)(2,1)} %q_ref.7, bf16[2048,512]{1,0:T(8,128)(2,1)} %kn_ref.7, bf16[2048,512]{1,0:T(8,128)(2,1)} %kn_ref.7, bf16[2048,512]{1,0:T(8,128)(2,1)} %kn_ref.7, bf16[2048,512]{1,0:T(8,128)(2,1)} %vn_ref.7, bf16[2048,512]{1,0:T(8,128)(2,1)} %vn_ref.7, ...), custom_call_target="tpu_custom_call" | custom-call | flops 20000000000 | bytes 70000000 | tf_op jit(solution)/shard_map/attend/pallas_call | solution.py:222
  41.1 0.1 collective-permute-start.7
  41.2 4.0 %attend.7 = bf16[512,512]{1,0:T(8,128)(2,1)S(1)} custom-call(s32[9]{0:T(128)S(1)} %stack.39.info, bf16[2048,512]{1,0:T(8,128)(2,1)} %q_ref.7, bf16[2048,512]{1,0:T(8,128)(2,1)} %kn_ref.7, bf16[2048,512]{1,0:T(8,128)(2,1)} %kn_ref.7, bf16[2048,512]{1,0:T(8,128)(2,1)} %kn_ref.7, bf16[2048,512]{1,0:T(8,128)(2,1)} %vn_ref.7, bf16[2048,512]{1,0:T(8,128)(2,1)} %vn_ref.7, ...), custom_call_target="tpu_custom_call" | custom-call | flops 20000000000 | bytes 70000000 | tf_op jit(solution)/shard_map/attend/pallas_call | solution.py:222
  45.2 2.5 %collective-permute-start.8 = (bf16[512,512]{1,0:T(8,128)(2,1)S(1)}, bf16[512,512]{1,0:T(8,128)(2,1)S(1)}, u32[]{:S(2)}, u32[]{:S(2)}) collective-permute-start(bf16[512,512]{1,0:T(8,128)(2,1)S(1)} %attend.7), channel_id=1, source_target_pairs={{0,1},{1,0},{2,3},{3,2},{4,5},{5,4},{6,7},{7,6},{8,9},{9,8},{10,11... | collective-permute-start | bytes 1572872 | tf_op jit(solution)/shard_map/ppermute | solution.py:289
  47.7 4.0 %attend.4 = bf16[512,512]{1,0:T(8,128)(2,1)S(1)} custom-call(s32[9]{0:T(128)S(1)} %stack.39.info, bf16[2048,512]{1,0:T(8,128)(2,1)} %q_ref.7, bf16[2048,512]{1,0:T(8,128)(2,1)} %kn_ref.7, bf16[2048,512]{1,0:T(8,128)(2,1)} %kn_ref.7, bf16[2048,512]{1,0:T(8,128)(2,1)} %kn_ref.7, bf16[2048,512]{1,0:T(8,128)(2,1)} %vn_ref.7, bf16[2048,512]{1,0:T(8,128)(2,1)} %vn_ref.7, ...), custom_call_target="tpu_custom_call" | custom-call | flops 20000000000 | bytes 70000000 | tf_op jit(solution)/shard_map/attend/pallas_call | solution.py:222
  51.7 1.6 %collective-permute-start.5 = (bf16[512,512]{1,0:T(8,128)(2,1)S(1)}, bf16[512,512]{1,0:T(8,128)(2,1)S(1)}, u32[]{:S(2)}, u32[]{:S(2)}) collective-permute-start(bf16[512,512]{1,0:T(8,128)(2,1)S(1)} %attend.4), channel_id=1, source_target_pairs={{0,3},{1,2},{2,1},{3,0},{4,7},{5,6},{6,5},{7,4},{8,11},{9,10},{10,... | collective-permute-start | bytes 1572872 | tf_op jit(solution)/shard_map/ppermute | solution.py:289
  53.3 0.5 collective-permute-start.3
  53.7 4.0 %attend.5.refs_3_ = bf16[512,512]{1,0:T(8,128)(2,1)S(1)} custom-call(s32[9]{0:T(128)S(1)} %stack.39.info, bf16[2048,512]{1,0:T(8,128)(2,1)} %q_ref.7, bf16[2048,512]{1,0:T(8,128)(2,1)} %kn_ref.7, bf16[2048,512]{1,0:T(8,128)(2,1)} %kn_ref.7, bf16[2048,512]{1,0:T(8,128)(2,1)} %kn_ref.7, bf16[2048,512]{1,0:T(8,128)(2,1)} %vn_ref.7, bf16[2048,512]{1,0:T(8,128)(2,1)} %vn_ref.7, ...), custom_call_target="tpu_custom_call" | custom-call | flops 20000000000 | bytes 70000000 | tf_op jit(solution)/shard_map/attend/pallas_call | solution.py:222
  57.7 0.0 collective-permute-done.6.refs_2_
  57.7 0.0 collective-permute-done.7.refs_4_
  57.7 0.0 collective-permute-done.8.refs_5_
  57.7 5.5 %project.2.refs_2_ = f32[512,2048]{1,0:T(8,128)S(1)} custom-call(bf16[512,2048]{1,0:T(8,128)(2,1)S(1)} %copy-done.1, bf16[512,2048]{1,0:T(8,128)(2,1)} %collective-permute-done.refs_1_, bf16[512,2048]{1,0:T(8,128)(2,1)} %collective-permute-done.6.refs_2_, bf16[512,512]{1,0:T(8,128)(2,1)S(1)} %attend.5.refs_3_, ...), custom_call_target="tpu_custom_call" | custom-call | flops 20000000000 | bytes 70000000 | tf_op jit(solution)/shard_map/project/pallas_call | solution.py:263
  63.3 2.8 %collective-permute-done.5.refs_1_ = bf16[512,512]{1,0:T(8,128)(2,1)S(1)} collective-permute-done((bf16[512,512]{1,0:T(8,128)(2,1)S(1)}, bf16[512,512]{1,0:T(8,128)(2,1)S(1)}, u32[]{:S(2)}, u32[]{:S(2)}) %collective-permute-start.5) | collective-permute-done | bytes 524320 | tf_op jit(solution)/shard_map/ppermute | solution.py:289
  66.0 0.0 collective-permute-done.3.refs_0_
  66.0 2.9 %project.3 = bf16[512,2048]{1,0:T(8,128)(2,1)} custom-call(bf16[512,2048]{1,0:T(8,128)(2,1)S(1)} %collective-permute-done.3.refs_0_, bf16[512,512]{1,0:T(8,128)(2,1)S(1)} %collective-permute-done.5.refs_1_, f32[512,2048]{1,0:T(8,128)S(1)} %project.2.refs_2_), custom_call_target="tpu_custom_call" | custom-call | flops 20000000000 | bytes 70000000 | tf_op jit(solution)/shard_map/project/pallas_call | solution.py:263
  (2 shorter events, 0.0 us)
Async XLA Ops:
  0.0 29.4 %collective-permute-start = (bf16[512,2048]{1,0:T(8,128)(2,1)}, bf16[512,2048]{1,0:T(8,128)(2,1)}, u32[]{:S(2)}, u32[]{:S(2)}) collective-permute-start(bf16[512,2048]{1,0:T(8,128)(2,1)} %refs_0_.1), channel_id=1, source_target_pairs={{0,2},{1,35},{2,0},{3,33},{4,6},{5,39},{6,4},{7,37},{8,10},{9,43},... | collective-permute-start | bytes 6291464 | tf_op jit(solution)/shard_map/ppermute | solution.py:296
  3.6 1.6 %copy-start = (bf16[2048,512]{1,0:T(8,128)(2,1)S(1)}, bf16[2048,512]{1,0:T(8,128)(2,1)}, u32[]{:S(2)}) copy-start(bf16[2048,512]{1,0:T(8,128)(2,1)} %kn_ref.7) | copy-start | bytes 6291460
  7.7 18.3 %copy-start.1 = (bf16[512,2048]{1,0:T(8,128)(2,1)S(1)}, bf16[512,2048]{1,0:T(8,128)(2,1)}, u32[]{:S(2)}) copy-start(bf16[512,2048]{1,0:T(8,128)(2,1)} %refs_0_.1) | copy-start | bytes 6291460
  7.7 5.1 %collective-permute-start.1 = (bf16[96,512]{1,0:T(8,128)(2,1)S(1)}, bf16[96,512]{1,0:T(8,128)(2,1)S(1)}, u32[]{:S(2)}, u32[]{:S(2)}) collective-permute-start(bf16[96,512]{1,0:T(8,128)(2,1)S(1)} %get-tuple-element.12.own_ref), channel_id=1, source_target_pairs={{0,4},{4,0},{8,12},{12,8},{16,20},{20,16},{24,28},{28,24},{32,36},... | collective-permute-start | bytes 294920 | tf_op jit(solution)/shard_map/ppermute | solution.py:286
  13.5 12.2 %collective-permute-start.2 = (bf16[96,512]{1,0:T(8,128)(2,1)S(1)}, bf16[96,512]{1,0:T(8,128)(2,1)S(1)}, u32[]{:S(2)}, u32[]{:S(2)}) collective-permute-start(bf16[96,512]{1,0:T(8,128)(2,1)S(1)} %get-tuple-element.14.mid_ref), channel_id=1, source_target_pairs={{0,252},{4,8},{8,4},{12,16},{16,12},{20,24},{24,20},{28,32},{32,28... | collective-permute-start | bytes 294920 | tf_op jit(solution)/shard_map/ppermute | solution.py:286
  20.1 17.0 %all-to-all-start = ((bf16[32,2,512]{2,1,0:T(2,128)(2,1)}), bf16[32,2,512]{2,1,0:T(2,128)(2,1)S(1)}, u32[]{:S(2)}, u32[]{:S(2)}) async-start(bf16[32,2,512]{2,1,0:T(2,128)(2,1)} %get-tuple-element.18), calls=%async_computation | async-start | bytes 131072 | tf_op jit(solution)/shard_map/all_to_all | solution.py:310
  25.7 11.3 %collective-permute-start.4 = (bf16[32,512]{1,0:T(8,128)(2,1)S(1)}, bf16[32,512]{1,0:T(8,128)(2,1)S(1)}, u32[]{:S(2)}, u32[]{:S(2)}) collective-permute-start(bf16[32,512]{1,0:T(8,128)(2,1)S(1)} %slice.4), channel_id=1, source_target_pairs={{0,4},{4,0},{8,12},{12,8},{16,20},{20,16},{24,28},{28,24},{32,36},... | collective-permute-start | bytes 98312 | tf_op jit(solution)/shard_map/ppermute | solution.py:286
  26.0 31.7 %collective-permute-start.6 = (bf16[512,2048]{1,0:T(8,128)(2,1)S(1)}, bf16[512,2048]{1,0:T(8,128)(2,1)}, u32[]{:S(2)}, u32[]{:S(2)}) collective-permute-start(bf16[512,2048]{1,0:T(8,128)(2,1)S(1)} %copy-done.1), channel_id=1, source_target_pairs={{0,1},{1,0},{2,3},{3,2},{4,5},{5,4},{6,7},{7,6},{8,9},{9,8},{10,11... | collective-permute-start | bytes 6291464 | tf_op jit(solution)/shard_map/ppermute | solution.py:289
  41.1 16.6 %collective-permute-start.7 = (bf16[512,512]{1,0:T(8,128)(2,1)S(1)}, bf16[512,512]{1,0:T(8,128)(2,1)S(1)}, u32[]{:S(2)}, u32[]{:S(2)}) collective-permute-start(bf16[512,512]{1,0:T(8,128)(2,1)S(1)} %attend.6), channel_id=1, source_target_pairs={{0,2},{1,3},{2,0},{3,1},{4,6},{5,7},{6,4},{7,5},{8,10},{9,11},{10,... | collective-permute-start | bytes 1572872 | tf_op jit(solution)/shard_map/ppermute | solution.py:289
  45.2 12.5 %collective-permute-start.8 = (bf16[512,512]{1,0:T(8,128)(2,1)S(1)}, bf16[512,512]{1,0:T(8,128)(2,1)S(1)}, u32[]{:S(2)}, u32[]{:S(2)}) collective-permute-start(bf16[512,512]{1,0:T(8,128)(2,1)S(1)} %attend.7), channel_id=1, source_target_pairs={{0,1},{1,0},{2,3},{3,2},{4,5},{5,4},{6,7},{7,6},{8,9},{9,8},{10,11... | collective-permute-start | bytes 1572872 | tf_op jit(solution)/shard_map/ppermute | solution.py:289
  51.7 14.4 %collective-permute-start.5 = (bf16[512,512]{1,0:T(8,128)(2,1)S(1)}, bf16[512,512]{1,0:T(8,128)(2,1)S(1)}, u32[]{:S(2)}, u32[]{:S(2)}) collective-permute-start(bf16[512,512]{1,0:T(8,128)(2,1)S(1)} %attend.4), channel_id=1, source_target_pairs={{0,3},{1,2},{2,1},{3,0},{4,7},{5,6},{6,5},{7,4},{8,11},{9,10},{10,... | collective-permute-start | bytes 1572872 | tf_op jit(solution)/shard_map/ppermute | solution.py:289
  53.3 12.8 %collective-permute-start.3 = (bf16[512,2048]{1,0:T(8,128)(2,1)}, bf16[512,2048]{1,0:T(8,128)(2,1)S(1)}, u32[]{:S(2)}, u32[]{:S(2)}) collective-permute-start(bf16[512,2048]{1,0:T(8,128)(2,1)} %collective-permute-done.refs_1_), channel_id=1, source_target_pairs={{0,1},{1,0},{2,3},{3,2},{4,5},{5,4},{6,7},{7,6},{8,9},{9,8},{10,11... | collective-permute-start | bytes 6291464 | tf_op jit(solution)/shard_map/ppermute | solution.py:289

commit v3 on v2

--- a/solution.py
+++ b/solution.py
@@ -15,9 +15,9 @@
 NEG = -1e30
 F32 = jnp.float32
 BF16 = jnp.bfloat16
-POOL_VMEM, ATTEND_VMEM, PROJECT_VMEM = (mib * 1024 * 1024 for mib in (51, 51, 24))
+POOL_VMEM, ATTEND_VMEM, PROJECT_VMEM = (mib * 1024 * 1024 for mib in (53, 51, 24))
 CHUNKS = 4
-ORDER = ((0, 2), (1, 1), (2, 3), (3, 0))
+ATTEND_COST = pl.CostEstimate(flops=20000000000, bytes_accessed=70000000, transcendentals=0)
 SMALL = pl.CostEstimate(flops=1000, bytes_accessed=1000, transcendentals=0)
 
 TK, TV, AK, AV, BK, BV = (16 * i for i in range(6))
@@ -95,7 +95,8 @@
         rows = slice(at, at + 16)
         pair = own_ref[rows, :].astype(F32) + near_ref[rows, :].astype(F32)
         to_far_ref[rows, :] = pair.astype(BF16)
-        means.append(jnp.sum(pair, axis=0, keepdims=True) * 0.0625)
+        mean = jnp.sum(pair, axis=0, keepdims=True) * 0.0625
+        means += [mean[:, HD * head : HD * head + HD] for head in range(HEADS)]
     both = jnp.concatenate(means, axis=0).astype(BF16)
     l3_ref[...] = jnp.broadcast_to(both[None], l3_ref.shape)
 
@@ -105,7 +106,7 @@
         middle_kernel,
         out_shape=[
             jax.ShapeDtypeStruct((96, WIDE), BF16),
-            jax.ShapeDtypeStruct((copies, 2, WIDE), BF16),
+            jax.ShapeDtypeStruct((copies, 2 * HEADS, HD), BF16),
         ],
         cost_estimate=pl.CostEstimate(flops=1000000000, bytes_accessed=3500000, transcendentals=0),
         compiler_params=pltpu.CompilerParams(vmem_limit_bytes=4 * 1024 * 1024),
@@ -130,13 +131,22 @@
             l1x[which, 0:16, :] = jnp.where(odd == 1, near, far)
             l1x[which, 16:144, :] = l1_ref[which]
             l1x[which, 144:160, :] = jnp.where(odd == 1, far, near)
+        parts = 2 * HEADS * l3_ref.shape[0]
+        wanted = lax.broadcasted_iota(jnp.int32, (parts, parts), 0)
+        given = lax.broadcasted_iota(jnp.int32, (parts, parts), 1)
+        pick = given == 2 * HEADS * (wanted % 32) + wanted // 32
+        level3 = jnp.dot(
+            jnp.where(pick, 1.0, 0.0).astype(BF16),
+            l3_ref[...].reshape(parts, HD),
+            preferred_element_type=F32,
+        ).astype(BF16)
         for scratch, at, which in ((sk, BK, 0), (sv, BV, 1)):
             scratch[48:64, :] = mid_ref[at : at + 16, :]
             scratch[64:80, :] = far_ref[at : at + 16, :]
             scratch[80:96, :] = farther_ref[at - BK : at - BK + 16, :]
-            here = lax.broadcasted_iota(jnp.int32, (32, 2, WIDE), 1) == which
-            picked = jnp.sum(jnp.where(here, l3_ref[...].astype(F32), 0.0), axis=1)
-            scratch[96:128, :] = picked.astype(BF16)
+            for head in range(HEADS):
+                first = 32 * (HEADS * which + head)
+                scratch[96:128, HD * head : HD * head + HD] = level3[first : first + 32, :]
         zeros = jnp.zeros((32, WIDE), BF16)
         kx[288:320, :] = zeros
         vx[288:320, :] = zeros
@@ -200,7 +210,7 @@
         out_ref[rows[part], cols[head]] = (value * (1.0 / sum_)).astype(BF16)
 
 
-def attend(total, base, info, queries, keys, values, l1, mid, near, far, farther, l3):
+def windows(base):
     def main(i, s):
         return (s[1 + base + i], 0)
 
@@ -209,23 +219,25 @@
 
     def after(i, s):
         return (jnp.minimum(16 * s[1 + base + i] + 16, 127), 0)
-
-    def whole(array):
-        return pl.BlockSpec(array.shape, lambda i, s: (0,) * array.ndim)
 
     wide, thin_low, thin_high = (
         pl.BlockSpec((256, WIDE), main),
         pl.BlockSpec((16, WIDE), before),
         pl.BlockSpec((16, WIDE), after),
     )
-    small = (l1, mid, near, far, farther, l3)
+    return [wide, wide, thin_low, thin_high, wide, thin_low, thin_high]
+
+
+def attend(total, base, steps, info, rows, small):
+    def whole(array):
+        return pl.BlockSpec(array.shape, lambda i, s: (0,) * array.ndim)
+
     return pl.pallas_call(
         functools.partial(attend_kernel, total, base),
         grid_spec=pltpu.PrefetchScalarGridSpec(
             num_scalar_prefetch=1,
-            grid=(2,),
-            in_specs=[wide, wide, thin_low, thin_high, wide, thin_low, thin_high]
-            + [whole(array) for array in small],
+            grid=(steps,),
+            in_specs=windows(base) + [whole(array) for array in small],
             out_specs=pl.BlockSpec((256, WIDE), lambda i, s: (i, 0)),
             scratch_shapes=[
                 pltpu.VMEM((320, WIDE), BF16),
@@ -235,16 +247,26 @@
                 pltpu.VMEM((128, WIDE), BF16),
             ],
         ),
-        out_shape=jax.ShapeDtypeStruct((512, WIDE), BF16),
-        cost_estimate=pl.CostEstimate(flops=20000000000, bytes_accessed=70000000, transcendentals=0),
+        out_shape=jax.ShapeDtypeStruct((256 * steps, WIDE), BF16),
+        cost_estimate=ATTEND_COST,
         compiler_params=pltpu.CompilerParams(vmem_limit_bytes=ATTEND_VMEM),
         name="attend",
-    )(info, queries, keys, keys, keys, values, values, values, *small)
-
-
-def project_kernel(n, m, *refs):
-    weights, attended, before, out_ref = refs[:m], refs[m : n + m], refs[n + m : -1], refs[-1]
-    left = jnp.concatenate([a[...] for a in attended], axis=1)
+    )(info, *rows, *small)
+
+
+def project_kernel(ahead, n, m, *refs):
+    refs = refs[ahead:]
+    before, weights, attended, out_ref = refs[: -n - m - 1], refs[-n - m - 1 : -n - 1], refs[-n - 1 : -1], refs[-1]
+    whole, halves = [], []
+    for a in attended:
+        if a.shape[0] == out_ref.shape[0]:
+            whole.append(a[...])
+        else:
+            halves.append(a[...])
+            if len(halves) == 2:
+                whole.append(jnp.concatenate(halves, axis=0))
+                halves = []
+    left = jnp.concatenate(whole, axis=1)
     right = jnp.concatenate([w[...] for w in weights], axis=0)
     total = jnp.dot(left, right, preferred_element_type=F32)
     if before:
@@ -252,28 +274,29 @@
     out_ref[...] = total.astype(out_ref.dtype)
 
 
-def project(attended, weights, before, dtype):
+def project(attended, weights, before, dtype, ahead=()):
     rows, columns = attended[0].shape[0], weights[0].shape[1]
     tile = 1024
-    depth = WIDE * len(attended)
+    depth = sum(w.shape[0] for w in weights)
 
     def tiles(arrays):
         return [pl.BlockSpec((w.shape[0], tile), lambda i: (0, i)) for w in arrays]
 
     return pl.pallas_call(
-        functools.partial(project_kernel, len(attended), len(weights)),
+        functools.partial(project_kernel, len(ahead), len(attended), len(weights)),
         grid=(columns // tile,),
         in_specs=[
+            *(pl.BlockSpec(memory_space=pl.ANY) for _ in ahead),
+            *tiles(before),
             *tiles(weights),
             *(pl.BlockSpec(a.shape, lambda i: (0, 0)) for a in attended),
-            *tiles(before),
         ],
         out_specs=pl.BlockSpec((rows, tile), lambda i: (0, i)),
         out_shape=jax.ShapeDtypeStruct((rows, columns), dtype),
         cost_estimate=pl.CostEstimate(flops=20000000000, bytes_accessed=70000000, transcendentals=0),
         compiler_params=pltpu.CompilerParams(vmem_limit_bytes=PROJECT_VMEM),
         name="project",
-    )(*weights, *attended, *before)
+    )(*ahead, *before, *weights, *attended)
 
 
 def body(queries, keys, values, out_weight):
@@ -295,7 +318,7 @@
                 pairs.append((4 * i + j, 4 * (i ^ 8 if j % 2 else i) + (j ^ 2)))
         return lax.ppermute(array, ("seq", "head"), pairs)
 
-    order = (2, 1, 3, 0)
+    order = (2, 3, 1, 0)
     groups = [2 * (h ^ bit) + part for bit in order for part in range(2)]
     info = jnp.stack([s, *groups]).astype(jnp.int32)
 
@@ -305,19 +328,21 @@
     near = permute(to_near, lambda i: i ^ 1)
     to_far, l3 = middle(to_near, near, to_far, blocks // 2)
     far = permute(to_far, lambda i: i + 1 if i % 2 else i - 1)
-    farther = permute(far[BK:, :], lambda i: i ^ 1)
+    farther = permute(to_far[BK:, :], lambda i: i + 2 if i % 2 else i - 2)
     peers = [[2 * i + parity for i in range(blocks // 2)] for parity in range(2)]
     l3 = lax.all_to_all(l3, "seq", 0, 0, axis_index_groups=peers)
 
-    w_far, far = lax.optimization_barrier((w_far, far))
+    w_far, w_near, far = lax.optimization_barrier((w_far, w_near, far))
     w_cross = swap(w_far, 1)
-    outs = {}
-    for at, bit in ORDER:
-        part = attend(total, 2 * at, info, queries, keys, values, l1, to_far, near, far, farther, l3)
-        outs[bit] = swap(part, bit) if bit else part
-
-    inner = project([outs[0], outs[2], outs[1]], [out_weight, w_far, w_near], [], F32)
-    return project([outs[3]], [w_cross], [inner], BF16)
+    rows = (queries, keys, keys, keys, values, values, values)
+    small = (l1, to_far, near, far, farther, l3)
+    foreign = [swap(attend(total, part, 1, info, rows, small), 2) for part in range(2)]
+    last = swap(attend(total, 2, 2, info, rows, small), 3)
+    inside = swap(attend(total, 4, 2, info, rows, small), 1)
+    own = attend(total, 6, 2, info, rows, small)
+
+    inner = project([own, *foreign, inside], [out_weight, w_far, w_near], [], F32)
+    return project([last], [w_cross], [inner], BF16, [*foreign, last])
 
 
 def solution(mesh):

time: 69.2 us -> 66.4 us (0.960)
  waiting for transfers between devices: 14.8 us -> 5.26 us
  starting transfers between devices: 24.8 us -> 33.1 us
  local copies, waits for them, and re-layouts: 1.69 us -> 0.1 us
    all_to_all x1, waiting for transfers between devices: 7.68 us -> 0.01 us  [body(): l3 = lax.all_to_all(l3, 'seq', 0, 0, axis_index_groups=peers)]
    all_to_all x1, starting transfers between devices: 5.58 us -> 13.1 us  [body(): l3 = lax.all_to_all(l3, 'seq', 0, 0, axis_index_groups=peers)]
    ppermute x3, starting transfers between devices: 8.58 us -> 11.4 us  [permute(): lax.ppermute(array, 'seq', [(i, move(i) % blocks) for i in range(blocks)])]
    ppermute x5 -> x6, starting transfers between devices: 7.08 us -> 5.04 us  [swap(): return lax.ppermute(array, 'head', [(i, i ^ bit) for i in range(4)])]
    ppermute x5 -> x6, waiting for transfers between devices: 2.79 us -> 0.77 us  [swap(): return lax.ppermute(array, 'head', [(i, i ^ bit) for i in range(4)])]
    unnamed x4, local copies, waits for them, and re-layouts: 1.6 us -> 0.01 us
    ppermute x3, waiting for transfers between devices: 3.43 us -> 4.49 us  [permute(): lax.ppermute(array, 'seq', [(i, move(i) % blocks) for i in range(blocks)])]
    ppermute x1, waiting for transfers between devices: 0.95 us -> 0.01 us  [cross(): return lax.ppermute(array, ('seq', 'head'), pairs)]
  transfers between devices with their start and end apart: 10 -> 11, of which waited for: 4 -> 4; matrix products, arithmetic and copies ran while one was open for 0% -> 0% of each run, Pallas kernels for 36% -> 34%
where the time goes in v3:
time: 66.4 us; the launch traced here: 66.2 us
  starting transfers between devices  33.1 us (50%)
  Pallas kernels  27.6 us (42%)
  waiting for transfers between devices  5.26 us (8%)
    pallas_call x5, Pallas kernels, attend(): pl.pallas_call(functools.partial(attend_kernel, total, base), grid_spec=p...  15.9 us
    all_to_all x1, starting transfers between devices, body(): l3 = lax.all_to_all(l3, 'seq', 0, 0, axis_index_groups=peers)  13.1 us
    ppermute x3, starting transfers between devices, permute(): lax.ppermute(array, 'seq', [(i, move(i) % blocks) for i in range(blocks)])  11.4 us
    pallas_call x2, Pallas kernels, project(): pl.pallas_call(functools.partial(project_kernel, len(ahead), len(attended...  8.39 us
    ppermute x6, starting transfers between devices, swap(): return lax.ppermute(array, 'head', [(i, i ^ bit) for i in range(4)])  5.04 us
    ppermute x3, waiting for transfers between devices, permute(): lax.ppermute(array, 'seq', [(i, move(i) % blocks) for i in range(blocks)])  4.49 us
    ppermute x1, starting transfers between devices, cross(): return lax.ppermute(array, ('seq', 'head'), pairs)  3.56 us
    pallas_call x1, Pallas kernels, pool(): pl.pallas_call(pool_kernel, in_specs=[pl.BlockSpec(memory_space=pltpu.HBM...  2.65 us
  transfers between devices with their start and end apart: 11, of which 4 were waited for; matrix products, arithmetic and copies ran while one was open for 0% of the time, Pallas kernels for 34%

profile of v3, /device:TPU:1, one launch (start us, length us, event | category | flops | bytes accessed | tf_op | source)
XLA Modules:
  0.0 66.2 jit_solution(4926688392503585816)
XLA Ops:
  0.0 3.6 %collective-permute-start.1 = (bf16[512,2048]{1,0:T(8,128)(2,1)}, bf16[512,2048]{1,0:T(8,128)(2,1)}, u32[]{:S(2)}, u32[]{:S(2)}) collective-permute-start(bf16[512,2048]{1,0:T(8,128)(2,1)} %refs_0_.1), channel_id=1, source_target_pairs={{0,2},{1,35},{2,0},{3,33},{4,6},{5,39},{6,4},{7,37},{8,10},{9,43},... | collective-permute-start | bytes 6291464 | tf_op jit(solution)/shard_map/ppermute | solution.py:319
  3.6 0.0 collective-permute-start.2
  3.6 2.6 %pool.1 = (bf16[2,128,512]{2,1,0:T(8,128)(2,1)S(1)}, bf16[96,512]{1,0:T(8,128)(2,1)S(1)}, bf16[64,512]{1,0:T(8,128)(2,1)S(1)}) custom-call(bf16[2048,512]{1,0:T(8,128)(2,1)} %kn_ref.9, bf16[2048,512]{1,0:T(8,128)(2,1)} %vn_ref.9), custom_call_target="tpu_custom_call" | custom-call | flops 4000000000 | bytes 14000000 | tf_op jit(solution)/shard_map/pool/pallas_call | solution.py:68
  6.2 0.0 copy-start
  6.2 1.7 %collective-permute-start = (bf16[96,512]{1,0:T(8,128)(2,1)S(1)}, bf16[96,512]{1,0:T(8,128)(2,1)S(1)}, u32[]{:S(2)}, u32[]{:S(2)}) collective-permute-start(bf16[96,512]{1,0:T(8,128)(2,1)S(1)} %get-tuple-element.14.own_ref), channel_id=1, source_target_pairs={{0,4},{4,0},{8,12},{12,8},{16,20},{20,16},{24,28},{28,24},{32,36},... | collective-permute-start | bytes 294920 | tf_op jit(solution)/shard_map/ppermute | solution.py:309
  8.0 2.7 %collective-permute-done.near_ref = bf16[96,512]{1,0:T(8,128)(2,1)S(1)} collective-permute-done((bf16[96,512]{1,0:T(8,128)(2,1)S(1)}, bf16[96,512]{1,0:T(8,128)(2,1)S(1)}, u32[]{:S(2)}, u32[]{:S(2)}) %collective-permute-start) | collective-permute-done | bytes 98336 | tf_op jit(solution)/shard_map/ppermute | solution.py:309
  10.7 0.7 middle.1
  11.3 13.1 %all-to-all-start = ((bf16[32,8,128]{2,1,0:T(8,128)(2,1)}), bf16[32,8,128]{2,1,0:T(8,128)(2,1)S(1)}, u32[]{:S(2)}, u32[]{:S(2)}) async-start(bf16[32,8,128]{2,1,0:T(8,128)(2,1)} %get-tuple-element.18), calls=%async_computation | async-start | bytes 131072 | tf_op jit(solution)/shard_map/all_to_all | solution.py:333
  24.4 7.6 %collective-permute-start.3 = (bf16[96,512]{1,0:T(8,128)(2,1)S(1)}, bf16[96,512]{1,0:T(8,128)(2,1)S(1)}, u32[]{:S(2)}, u32[]{:S(2)}) collective-permute-start(bf16[96,512]{1,0:T(8,128)(2,1)S(1)} %get-tuple-element.16.mid_ref), channel_id=1, source_target_pairs={{0,252},{4,8},{8,4},{12,16},{16,12},{20,24},{24,20},{28,32},{32,28... | collective-permute-start | bytes 294920 | tf_op jit(solution)/shard_map/ppermute | solution.py:309
  32.0 2.1 %collective-permute-start.4 = (bf16[32,512]{1,0:T(8,128)(2,1)S(1)}, bf16[32,512]{1,0:T(8,128)(2,1)S(1)}, u32[]{:S(2)}, u32[]{:S(2)}) collective-permute-start(bf16[32,512]{1,0:T(8,128)(2,1)S(1)} %slice.3), channel_id=1, source_target_pairs={{0,248},{4,12},{8,0},{12,20},{16,8},{20,28},{24,16},{28,36},{32,24... | collective-permute-start | bytes 98312 | tf_op jit(solution)/shard_map/ppermute | solution.py:309
  34.1 0.1 stack.39.info
  34.2 0.8 %collective-permute-done.3.far_ref = bf16[96,512]{1,0:T(8,128)(2,1)S(1)} collective-permute-done((bf16[96,512]{1,0:T(8,128)(2,1)S(1)}, bf16[96,512]{1,0:T(8,128)(2,1)S(1)}, u32[]{:S(2)}, u32[]{:S(2)}) %collective-permute-start.3) | collective-permute-done | bytes 98336 | tf_op jit(solution)/shard_map/ppermute | solution.py:309
  34.9 0.0 collective-permute-done.1.refs_1_
  34.9 0.0 collective-permute-done.2.refs_2_
  34.9 1.0 %collective-permute-done.4.farther_ref = bf16[32,512]{1,0:T(8,128)(2,1)S(1)} collective-permute-done((bf16[32,512]{1,0:T(8,128)(2,1)S(1)}, bf16[32,512]{1,0:T(8,128)(2,1)S(1)}, u32[]{:S(2)}, u32[]{:S(2)}) %collective-permute-start.4) | collective-permute-done | bytes 32800 | tf_op jit(solution)/shard_map/ppermute | solution.py:309
  36.0 2.4 %attend.5 = bf16[256,512]{1,0:T(8,128)(2,1)S(1)} custom-call(s32[9]{0:T(128)S(1)} %stack.39.info, bf16[2048,512]{1,0:T(8,128)(2,1)S(1)} %copy-done, bf16[2048,512]{1,0:T(8,128)(2,1)} %kn_ref.9, bf16[2048,512]{1,0:T(8,128)(2,1)} %kn_ref.9, bf16[2048,512]{1,0:T(8,128)(2,1)} %kn_ref.9, bf16[2048,512]{1,0:T(8,128)(2,1)} %vn_ref.9, bf16[2048,512]{1,0:T(8,128)(2,1)} %vn_ref.9, ...), custom_call_target="tpu_custom_call" | custom-call | flops 20000000000 | bytes 70000000 | tf_op jit(solution)/shard_map/attend/pallas_call | solution.py:235
  38.3 0.1 collective-permute-start.5
  38.4 2.4 %attend.6 = bf16[256,512]{1,0:T(8,128)(2,1)S(1)} custom-call(s32[9]{0:T(128)S(1)} %stack.39.info, bf16[2048,512]{1,0:T(8,128)(2,1)S(1)} %copy-done, bf16[2048,512]{1,0:T(8,128)(2,1)} %kn_ref.9, bf16[2048,512]{1,0:T(8,128)(2,1)} %kn_ref.9, bf16[2048,512]{1,0:T(8,128)(2,1)} %kn_ref.9, bf16[2048,512]{1,0:T(8,128)(2,1)} %vn_ref.9, bf16[2048,512]{1,0:T(8,128)(2,1)} %vn_ref.9, ...), custom_call_target="tpu_custom_call" | custom-call | flops 20000000000 | bytes 70000000 | tf_op jit(solution)/shard_map/attend/pallas_call | solution.py:235
  40.8 1.5 %collective-permute-start.6 = (bf16[256,512]{1,0:T(8,128)(2,1)S(1)}, bf16[256,512]{1,0:T(8,128)(2,1)S(1)}, u32[]{:S(2)}, u32[]{:S(2)}) collective-permute-start(bf16[256,512]{1,0:T(8,128)(2,1)S(1)} %attend.6), channel_id=1, source_target_pairs={{0,2},{1,3},{2,0},{3,1},{4,6},{5,7},{6,4},{7,5},{8,10},{9,11},{10,... | collective-permute-start | bytes 786440 | tf_op jit(solution)/shard_map/ppermute | solution.py:312
  42.4 3.7 %attend.7 = bf16[512,512]{1,0:T(8,128)(2,1)S(1)} custom-call(s32[9]{0:T(128)S(1)} %stack.39.info, bf16[2048,512]{1,0:T(8,128)(2,1)} %q_ref.9, bf16[2048,512]{1,0:T(8,128)(2,1)} %kn_ref.9, bf16[2048,512]{1,0:T(8,128)(2,1)} %kn_ref.9, bf16[2048,512]{1,0:T(8,128)(2,1)} %kn_ref.9, bf16[2048,512]{1,0:T(8,128)(2,1)} %vn_ref.9, bf16[2048,512]{1,0:T(8,128)(2,1)} %vn_ref.9, ...), custom_call_target="tpu_custom_call" | custom-call | flops 20000000000 | bytes 70000000 | tf_op jit(solution)/shard_map/attend/pallas_call | solution.py:235
  46.1 2.8 %collective-permute-start.7 = (bf16[512,512]{1,0:T(8,128)(2,1)S(1)}, bf16[512,512]{1,0:T(8,128)(2,1)S(1)}, u32[]{:S(2)}, u32[]{:S(2)}) collective-permute-start(bf16[512,512]{1,0:T(8,128)(2,1)S(1)} %attend.7), channel_id=1, source_target_pairs={{0,3},{1,2},{2,1},{3,0},{4,7},{5,6},{6,5},{7,4},{8,11},{9,10},{10,... | collective-permute-start | bytes 1572872 | tf_op jit(solution)/shard_map/ppermute | solution.py:312
  48.8 3.7 %attend.9 = bf16[512,512]{1,0:T(8,128)(2,1)S(1)} custom-call(s32[9]{0:T(128)S(1)} %stack.39.info, bf16[2048,512]{1,0:T(8,128)(2,1)} %q_ref.9, bf16[2048,512]{1,0:T(8,128)(2,1)} %kn_ref.9, bf16[2048,512]{1,0:T(8,128)(2,1)} %kn_ref.9, bf16[2048,512]{1,0:T(8,128)(2,1)} %kn_ref.9, bf16[2048,512]{1,0:T(8,128)(2,1)} %vn_ref.9, bf16[2048,512]{1,0:T(8,128)(2,1)} %vn_ref.9, ...), custom_call_target="tpu_custom_call" | custom-call | flops 20000000000 | bytes 70000000 | tf_op jit(solution)/shard_map/attend/pallas_call | solution.py:235
  52.6 0.0 copy-start.1
  52.6 0.4 collective-permute-start.8
  53.0 0.3 collective-permute-start.9
  53.2 3.7 %attend.8.refs_3_ = bf16[512,512]{1,0:T(8,128)(2,1)S(1)} custom-call(s32[9]{0:T(128)S(1)} %stack.39.info, bf16[2048,512]{1,0:T(8,128)(2,1)} %q_ref.9, bf16[2048,512]{1,0:T(8,128)(2,1)} %kn_ref.9, bf16[2048,512]{1,0:T(8,128)(2,1)} %kn_ref.9, bf16[2048,512]{1,0:T(8,128)(2,1)} %kn_ref.9, bf16[2048,512]{1,0:T(8,128)(2,1)} %vn_ref.9, bf16[2048,512]{1,0:T(8,128)(2,1)} %vn_ref.9, ...), custom_call_target="tpu_custom_call" | custom-call | flops 20000000000 | bytes 70000000 | tf_op jit(solution)/shard_map/attend/pallas_call | solution.py:235
  57.0 0.0 collective-permute-done.6.refs_5_.refs_1_
  57.0 0.0 collective-permute-done.8.refs_6_
  57.0 5.5 %project.2.refs_3_ = f32[512,2048]{1,0:T(8,128)S(1)} custom-call(bf16[512,2048]{1,0:T(8,128)(2,1)S(1)} %copy-done.1, bf16[512,2048]{1,0:T(8,128)(2,1)} %collective-permute-done.1.refs_1_, bf16[512,2048]{1,0:T(8,128)(2,1)} %collective-permute-done.2.refs_2_, bf16[512,512]{1,0:T(8,128)(2,1)S(1)} %attend.8.refs_3_, ...), custom_call_target="tpu_custom_call" | custom-call | flops 20000000000 | bytes 70000000 | tf_op jit(solution)/shard_map/project/pallas_call | solution.py:285
  62.6 0.8 %collective-permute-done.7.refs_2_.refs_5_ = bf16[512,512]{1,0:T(8,128)(2,1)S(1)} collective-permute-done((bf16[512,512]{1,0:T(8,128)(2,1)S(1)}, bf16[512,512]{1,0:T(8,128)(2,1)S(1)}, u32[]{:S(2)}, u32[]{:S(2)}) %collective-permute-start.7) | collective-permute-done | bytes 524320 | tf_op jit(solution)/shard_map/ppermute | solution.py:312
  63.3 0.0 collective-permute-done.9.refs_4_
  63.3 2.9 %project.3 = bf16[512,2048]{1,0:T(8,128)(2,1)} custom-call(bf16[256,512]{1,0:T(8,128)(2,1)S(1)} %collective-permute-done.5.refs_4_.refs_0_, bf16[256,512]{1,0:T(8,128)(2,1)S(1)} %collective-permute-done.6.refs_5_.refs_1_, bf16[512,512]{1,0:T(8,128)(2,1)S(1)} %collective-permute-done.7.refs_2_.refs_5_, f32[512,2048]{1,0:T(8,128)S(1)} %project.2.refs_3_, ...), custom_call_target="tpu_custom_call" | custom-call | flops 20000000000 | bytes 70000000 | tf_op jit(solution)/shard_map/project/pallas_call | solution.py:285
  (5 shorter events, 0.0 us)
Async XLA Ops:
  0.0 34.9 %collective-permute-start.1 = (bf16[512,2048]{1,0:T(8,128)(2,1)}, bf16[512,2048]{1,0:T(8,128)(2,1)}, u32[]{:S(2)}, u32[]{:S(2)}) collective-permute-start(bf16[512,2048]{1,0:T(8,128)(2,1)} %refs_0_.1), channel_id=1, source_target_pairs={{0,2},{1,35},{2,0},{3,33},{4,6},{5,39},{6,4},{7,37},{8,10},{9,43},... | collective-permute-start | bytes 6291464 | tf_op jit(solution)/shard_map/ppermute | solution.py:319
  3.6 31.4 %collective-permute-start.2 = (bf16[512,2048]{1,0:T(8,128)(2,1)}, bf16[512,2048]{1,0:T(8,128)(2,1)}, u32[]{:S(2)}, u32[]{:S(2)}) collective-permute-start(bf16[512,2048]{1,0:T(8,128)(2,1)} %refs_0_.1), channel_id=1, source_target_pairs={{0,1},{1,0},{2,3},{3,2},{4,5},{5,4},{6,7},{7,6},{8,9},{9,8},{10,11... | collective-permute-start | bytes 6291464 | tf_op jit(solution)/shard_map/ppermute | solution.py:312
  6.2 29.7 %copy-start = (bf16[2048,512]{1,0:T(8,128)(2,1)S(1)}, bf16[2048,512]{1,0:T(8,128)(2,1)}, u32[]{:S(2)}) copy-start(bf16[2048,512]{1,0:T(8,128)(2,1)} %q_ref.9) | copy-start | bytes 6291460
  6.2 4.4 %collective-permute-start = (bf16[96,512]{1,0:T(8,128)(2,1)S(1)}, bf16[96,512]{1,0:T(8,128)(2,1)S(1)}, u32[]{:S(2)}, u32[]{:S(2)}) collective-permute-start(bf16[96,512]{1,0:T(8,128)(2,1)S(1)} %get-tuple-element.14.own_ref), channel_id=1, source_target_pairs={{0,4},{4,0},{8,12},{12,8},{16,20},{20,16},{24,28},{28,24},{32,36},... | collective-permute-start | bytes 294920 | tf_op jit(solution)/shard_map/ppermute | solution.py:309
  11.3 24.6 %all-to-all-start = ((bf16[32,8,128]{2,1,0:T(8,128)(2,1)}), bf16[32,8,128]{2,1,0:T(8,128)(2,1)S(1)}, u32[]{:S(2)}, u32[]{:S(2)}) async-start(bf16[32,8,128]{2,1,0:T(8,128)(2,1)} %get-tuple-element.18), calls=%async_computation | async-start | bytes 131072 | tf_op jit(solution)/shard_map/all_to_all | solution.py:333
  24.4 10.5 %collective-permute-start.3 = (bf16[96,512]{1,0:T(8,128)(2,1)S(1)}, bf16[96,512]{1,0:T(8,128)(2,1)S(1)}, u32[]{:S(2)}, u32[]{:S(2)}) collective-permute-start(bf16[96,512]{1,0:T(8,128)(2,1)S(1)} %get-tuple-element.16.mid_ref), channel_id=1, source_target_pairs={{0,252},{4,8},{8,4},{12,16},{16,12},{20,24},{24,20},{28,32},{32,28... | collective-permute-start | bytes 294920 | tf_op jit(solution)/shard_map/ppermute | solution.py:309
  32.0 4.0 %collective-permute-start.4 = (bf16[32,512]{1,0:T(8,128)(2,1)S(1)}, bf16[32,512]{1,0:T(8,128)(2,1)S(1)}, u32[]{:S(2)}, u32[]{:S(2)}) collective-permute-start(bf16[32,512]{1,0:T(8,128)(2,1)S(1)} %slice.3), channel_id=1, source_target_pairs={{0,248},{4,12},{8,0},{12,20},{16,8},{20,28},{24,16},{28,36},{32,24... | collective-permute-start | bytes 98312 | tf_op jit(solution)/shard_map/ppermute | solution.py:309
  38.3 18.6 %collective-permute-start.5 = (bf16[256,512]{1,0:T(8,128)(2,1)S(1)}, bf16[256,512]{1,0:T(8,128)(2,1)S(1)}, u32[]{:S(2)}, u32[]{:S(2)}) collective-permute-start(bf16[256,512]{1,0:T(8,128)(2,1)S(1)} %attend.5), channel_id=1, source_target_pairs={{0,2},{1,3},{2,0},{3,1},{4,6},{5,7},{6,4},{7,5},{8,10},{9,11},{10,... | collective-permute-start | bytes 786440 | tf_op jit(solution)/shard_map/ppermute | solution.py:312
  40.8 16.2 %collective-permute-start.6 = (bf16[256,512]{1,0:T(8,128)(2,1)S(1)}, bf16[256,512]{1,0:T(8,128)(2,1)S(1)}, u32[]{:S(2)}, u32[]{:S(2)}) collective-permute-start(bf16[256,512]{1,0:T(8,128)(2,1)S(1)} %attend.6), channel_id=1, source_target_pairs={{0,2},{1,3},{2,0},{3,1},{4,6},{5,7},{6,4},{7,5},{8,10},{9,11},{10,... | collective-permute-start | bytes 786440 | tf_op jit(solution)/shard_map/ppermute | solution.py:312
  46.1 17.2 %collective-permute-start.7 = (bf16[512,512]{1,0:T(8,128)(2,1)S(1)}, bf16[512,512]{1,0:T(8,128)(2,1)S(1)}, u32[]{:S(2)}, u32[]{:S(2)}) collective-permute-start(bf16[512,512]{1,0:T(8,128)(2,1)S(1)} %attend.7), channel_id=1, source_target_pairs={{0,3},{1,2},{2,1},{3,0},{4,7},{5,6},{6,5},{7,4},{8,11},{9,10},{10,... | collective-permute-start | bytes 1572872 | tf_op jit(solution)/shard_map/ppermute | solution.py:312
  52.6 4.4 %copy-start.1 = (bf16[512,2048]{1,0:T(8,128)(2,1)S(1)}, bf16[512,2048]{1,0:T(8,128)(2,1)}, u32[]{:S(2)}) copy-start(bf16[512,2048]{1,0:T(8,128)(2,1)} %refs_0_.1) | copy-start | bytes 6291460
  52.6 4.4 %collective-permute-start.8 = (bf16[512,512]{1,0:T(8,128)(2,1)S(1)}, bf16[512,512]{1,0:T(8,128)(2,1)S(1)}, u32[]{:S(2)}, u32[]{:S(2)}) collective-permute-start(bf16[512,512]{1,0:T(8,128)(2,1)S(1)} %attend.9), channel_id=1, source_target_pairs={{0,1},{1,0},{2,3},{3,2},{4,5},{5,4},{6,7},{7,6},{8,9},{9,8},{10,11... | collective-permute-start | bytes 1572872 | tf_op jit(solution)/shard_map/ppermute | solution.py:312
  53.0 10.4 %collective-permute-start.9 = (bf16[512,2048]{1,0:T(8,128)(2,1)}, bf16[512,2048]{1,0:T(8,128)(2,1)S(1)}, u32[]{:S(2)}, u32[]{:S(2)}) collective-permute-start(bf16[512,2048]{1,0:T(8,128)(2,1)} %collective-permute-done.1.refs_1_), channel_id=1, source_target_pairs={{0,1},{1,0},{2,3},{3,2},{4,5},{5,4},{6,7},{7,6},{8,9},{9,8},{10,11... | collective-permute-start | bytes 6291464 | tf_op jit(solution)/shard_map/ppermute | solution.py:312

commit v4 on v3

--- a/solution.py
+++ b/solution.py
@@ -17,6 +17,7 @@
 BF16 = jnp.bfloat16
 POOL_VMEM, ATTEND_VMEM, PROJECT_VMEM = (mib * 1024 * 1024 for mib in (53, 51, 24))
 CHUNKS = 4
+PROJECT_COST = pl.CostEstimate(flops=20000000000, bytes_accessed=70000000, transcendentals=0)
 ATTEND_COST = pl.CostEstimate(flops=20000000000, bytes_accessed=70000000, transcendentals=0)
 SMALL = pl.CostEstimate(flops=1000, bytes_accessed=1000, transcendentals=0)
 
@@ -299,6 +300,39 @@
     )(*ahead, *before, *weights, *attended)
 
 
+def finish_kernel(ahead, *refs):
+    before, weight, attended, out, tiles, sems = refs[ahead:]
+    width = tiles.shape[2]
+    copies = []
+    for i in range(tiles.shape[0]):
+        cols = slice(width * i, width * i + width)
+        total = jnp.dot(attended[...], weight[:, cols], preferred_element_type=F32) + before[:, cols]
+        tiles[i] = total.astype(BF16)
+        copies.append(pltpu.make_async_copy(tiles.at[i], out.at[:, pl.ds(width * i, width)], sems.at[i]))
+        copies[-1].start()
+    for copy in copies:
+        copy.wait()
+
+
+def finish(attended, weight, before, ahead):
+    rows, columns = before.shape
+    tiles = 4
+    return pl.pallas_call(
+        functools.partial(finish_kernel, len(ahead)),
+        in_specs=[pl.BlockSpec(memory_space=pl.ANY) for _ in ahead]
+        + [pl.BlockSpec(memory_space=pltpu.VMEM)] * 3,
+        out_specs=pl.BlockSpec(memory_space=pl.ANY),
+        scratch_shapes=[
+            pltpu.VMEM((tiles, rows, columns // tiles), BF16),
+            pltpu.SemaphoreType.DMA((tiles,)),
+        ],
+        out_shape=jax.ShapeDtypeStruct((rows, columns), BF16),
+        cost_estimate=PROJECT_COST,
+        compiler_params=pltpu.CompilerParams(vmem_limit_bytes=PROJECT_VMEM),
+        name="finish",
+    )(*ahead, before, weight, attended)
+
+
 def body(queries, keys, values, out_weight):
     blocks = lax.axis_size("seq")
     total = queries.shape[0] * blocks
@@ -322,10 +356,11 @@
     groups = [2 * (h ^ bit) + part for bit in order for part in range(2)]
     info = jnp.stack([s, *groups]).astype(jnp.int32)
 
+    l1, to_near, to_far = pool(keys, values)
+    near = permute(to_near, lambda i: i ^ 1)
+    out_weight, l1 = lax.optimization_barrier((out_weight, l1))
     w_far = cross(out_weight)
     w_near = swap(out_weight, 1)
-    l1, to_near, to_far = pool(keys, values)
-    near = permute(to_near, lambda i: i ^ 1)
     to_far, l3 = middle(to_near, near, to_far, blocks // 2)
     far = permute(to_far, lambda i: i + 1 if i % 2 else i - 1)
     farther = permute(to_far[BK:, :], lambda i: i + 2 if i % 2 else i - 2)
@@ -342,7 +377,7 @@
     own = attend(total, 6, 2, info, rows, small)
 
     inner = project([own, *foreign, inside], [out_weight, w_far, w_near], [], F32)
-    return project([last], [w_cross], [inner], BF16, [*foreign, last])
+    return finish(last, w_cross, inner, [*foreign, last])
 
 
 def solution(mesh):

time: 66.4 us -> 64.9 us (0.977)
  starting transfers between devices: 33.1 us -> 32.4 us
    ppermute x6, starting transfers between devices: 5.04 us -> 9.29 us  [swap(): return lax.ppermute(array, 'head', [(i, i ^ bit) for i in range(4)])]
    pallas_call x2 -> x1, Pallas kernels: 8.39 us -> 5.78 us  [project(): pl.pallas_call(functools.partial(project_kernel, len(ahead), len(attended...]
    ppermute x1, starting transfers between devices: 3.56 us -> 1 us  [cross(): return lax.ppermute(array, ('seq', 'head'), pairs)]
    all_to_all x1, starting transfers between devices: 13.1 us -> 10.8 us  [body(): l3 = lax.all_to_all(l3, 'seq', 0, 0, axis_index_groups=peers)]
    pallas_call x0 -> x1, Pallas kernels: none -> 2.15 us  [finish(): pl.pallas_call(functools.partial(finish_kernel, len(ahead)), in_specs=[pl...]
    ppermute x6, waiting for transfers between devices: 0.77 us -> 0.02 us  [swap(): return lax.ppermute(array, 'head', [(i, i ^ bit) for i in range(4)])]
    ppermute x1, waiting for transfers between devices: 0.01 us -> 0.71 us  [cross(): return lax.ppermute(array, ('seq', 'head'), pairs)]
  transfers between devices with their start and end apart: 11 -> 11, of which waited for: 4 -> 4; matrix products, arithmetic and copies ran while one was open for 0% -> 0% of each run, Pallas kernels for 34% -> 31%
where the time goes in v4:
time: 64.9 us; the launch traced here: 64.6 us
  starting transfers between devices  32.4 us (50%)
  Pallas kernels  27.1 us (42%)
  waiting for transfers between devices  4.76 us (7%)
    pallas_call x5, Pallas kernels, attend(): pl.pallas_call(functools.partial(attend_kernel, total, base), grid_spec=p...  15.9 us
    ppermute x3, starting transfers between devices, permute(): lax.ppermute(array, 'seq', [(i, move(i) % blocks) for i in range(blocks)])  11.3 us
    all_to_all x1, starting transfers between devices, body(): l3 = lax.all_to_all(l3, 'seq', 0, 0, axis_index_groups=peers)  10.8 us
    ppermute x6, starting transfers between devices, swap(): return lax.ppermute(array, 'head', [(i, i ^ bit) for i in range(4)])  9.29 us
    pallas_call x1, Pallas kernels, project(): pl.pallas_call(functools.partial(project_kernel, len(ahead), len(attended...  5.78 us
    ppermute x3, waiting for transfers between devices, permute(): lax.ppermute(array, 'seq', [(i, move(i) % blocks) for i in range(blocks)])  4.04 us
    pallas_call x1, Pallas kernels, pool(): pl.pallas_call(pool_kernel, in_specs=[pl.BlockSpec(memory_space=pltpu.HBM...  2.65 us
    pallas_call x1, Pallas kernels, finish(): pl.pallas_call(functools.partial(finish_kernel, len(ahead)), in_specs=[pl...  2.15 us
  transfers between devices with their start and end apart: 11, of which 4 were waited for; matrix products, arithmetic and copies ran while one was open for 0% of the time, Pallas kernels for 31%

profile of v4, /device:TPU:1, one launch (start us, length us, event | category | flops | bytes accessed | tf_op | source)
XLA Modules:
  0.0 64.6 jit_solution(1343063323662931581)
XLA Ops:
  0.0 2.6 %pool.1 = (bf16[2,128,512]{2,1,0:T(8,128)(2,1)S(1)}, bf16[96,512]{1,0:T(8,128)(2,1)S(1)}, bf16[64,512]{1,0:T(8,128)(2,1)S(1)}) custom-call(bf16[2048,512]{1,0:T(8,128)(2,1)} %kn_ref.9, bf16[2048,512]{1,0:T(8,128)(2,1)} %vn_ref.9), custom_call_target="tpu_custom_call" | custom-call | flops 4000000000 | bytes 14000000 | tf_op jit(solution)/shard_map/pool/pallas_call | solution.py:69
  2.7 0.0 copy-start
  2.7 3.3 %collective-permute-start.2 = (bf16[512,2048]{1,0:T(8,128)(2,1)}, bf16[512,2048]{1,0:T(8,128)(2,1)}, u32[]{:S(2)}, u32[]{:S(2)}) collective-permute-start(bf16[512,2048]{1,0:T(8,128)(2,1)} %refs_0_), channel_id=1, source_target_pairs={{0,1},{1,0},{2,3},{3,2},{4,5},{5,4},{6,7},{7,6},{8,9},{9,8},{10,11... | collective-permute-start | bytes 6291464 | tf_op jit(solution)/shard_map/ppermute | solution.py:346
  6.0 1.0 %collective-permute-start.1 = (bf16[512,2048]{1,0:T(8,128)(2,1)}, bf16[512,2048]{1,0:T(8,128)(2,1)}, u32[]{:S(2)}, u32[]{:S(2)}) collective-permute-start(bf16[512,2048]{1,0:T(8,128)(2,1)} %refs_0_), channel_id=1, source_target_pairs={{0,2},{1,35},{2,0},{3,33},{4,6},{5,39},{6,4},{7,37},{8,10},{9,43},... | collective-permute-start | bytes 6291464 | tf_op jit(solution)/shard_map/ppermute | solution.py:353
  7.0 1.6 %collective-permute-start = (bf16[96,512]{1,0:T(8,128)(2,1)S(1)}, bf16[96,512]{1,0:T(8,128)(2,1)S(1)}, u32[]{:S(2)}, u32[]{:S(2)}) collective-permute-start(bf16[96,512]{1,0:T(8,128)(2,1)S(1)} %get-tuple-element.17.own_ref), channel_id=1, source_target_pairs={{0,4},{4,0},{8,12},{12,8},{16,20},{20,16},{24,28},{28,24},{32,36},... | collective-permute-start | bytes 294920 | tf_op jit(solution)/shard_map/ppermute | solution.py:343
  8.6 3.0 %collective-permute-done.near_ref = bf16[96,512]{1,0:T(8,128)(2,1)S(1)} collective-permute-done((bf16[96,512]{1,0:T(8,128)(2,1)S(1)}, bf16[96,512]{1,0:T(8,128)(2,1)S(1)}, u32[]{:S(2)}, u32[]{:S(2)}) %collective-permute-start) | collective-permute-done | bytes 98336 | tf_op jit(solution)/shard_map/ppermute | solution.py:343
  11.6 0.7 %middle.1 = (bf16[96,512]{1,0:T(8,128)(2,1)S(1)}, bf16[32,8,128]{2,1,0:T(8,128)(2,1)}) custom-call(bf16[96,512]{1,0:T(8,128)(2,1)S(1)} %get-tuple-element.17.own_ref, bf16[96,512]{1,0:T(8,128)(2,1)S(1)} %collective-permute-done.near_ref, bf16[64,512]{1,0:T(8,128)(2,1)S(1)} %get-tuple-element.18.far_ref), custom_call_target="tpu_custom_call" | custom-call | flops 1000000000 | bytes 3500000 | tf_op jit(solution)/shard_map/middle/pallas_call | solution.py:106
  12.2 10.8 %all-to-all-start = ((bf16[32,8,128]{2,1,0:T(8,128)(2,1)}), bf16[32,8,128]{2,1,0:T(8,128)(2,1)S(1)}, u32[]{:S(2)}, u32[]{:S(2)}) async-start(bf16[32,8,128]{2,1,0:T(8,128)(2,1)} %get-tuple-element.22), calls=%async_computation | async-start | bytes 131072 | tf_op jit(solution)/shard_map/all_to_all | solution.py:368
  23.0 7.6 %collective-permute-start.3 = (bf16[96,512]{1,0:T(8,128)(2,1)S(1)}, bf16[96,512]{1,0:T(8,128)(2,1)S(1)}, u32[]{:S(2)}, u32[]{:S(2)}) collective-permute-start(bf16[96,512]{1,0:T(8,128)(2,1)S(1)} %get-tuple-element.19.mid_ref), channel_id=1, source_target_pairs={{0,252},{4,8},{8,4},{12,16},{16,12},{20,24},{24,20},{28,32},{32,28... | collective-permute-start | bytes 294920 | tf_op jit(solution)/shard_map/ppermute | solution.py:343
  30.6 2.1 %collective-permute-start.4 = (bf16[32,512]{1,0:T(8,128)(2,1)S(1)}, bf16[32,512]{1,0:T(8,128)(2,1)S(1)}, u32[]{:S(2)}, u32[]{:S(2)}) collective-permute-start(bf16[32,512]{1,0:T(8,128)(2,1)S(1)} %slice.3), channel_id=1, source_target_pairs={{0,248},{4,12},{8,0},{12,20},{16,8},{20,28},{24,16},{28,36},{32,24... | collective-permute-start | bytes 98312 | tf_op jit(solution)/shard_map/ppermute | solution.py:343
  32.7 0.1 stack.39.info
  32.8 0.7 %collective-permute-done.3.far_ref = bf16[96,512]{1,0:T(8,128)(2,1)S(1)} collective-permute-done((bf16[96,512]{1,0:T(8,128)(2,1)S(1)}, bf16[96,512]{1,0:T(8,128)(2,1)S(1)}, u32[]{:S(2)}, u32[]{:S(2)}) %collective-permute-start.3) | collective-permute-done | bytes 98336 | tf_op jit(solution)/shard_map/ppermute | solution.py:343
  33.4 0.0 collective-permute-done.2.refs_2_
  33.4 0.7 %collective-permute-done.1.refs_1_ = bf16[512,2048]{1,0:T(8,128)(2,1)} collective-permute-done((bf16[512,2048]{1,0:T(8,128)(2,1)}, bf16[512,2048]{1,0:T(8,128)(2,1)}, u32[]{:S(2)}, u32[]{:S(2)}) %collective-permute-start.1) | collective-permute-done | bytes 2097184 | tf_op jit(solution)/shard_map/ppermute | solution.py:353
  34.2 0.4 collective-permute-done.4.farther_ref
  34.6 0.0 all-to-all-done.l3_ref
  34.6 2.4 %attend.5 = bf16[256,512]{1,0:T(8,128)(2,1)S(1)} custom-call(s32[9]{0:T(128)S(1)} %stack.39.info, bf16[2048,512]{1,0:T(8,128)(2,1)S(1)} %copy-done, bf16[2048,512]{1,0:T(8,128)(2,1)} %kn_ref.9, bf16[2048,512]{1,0:T(8,128)(2,1)} %kn_ref.9, bf16[2048,512]{1,0:T(8,128)(2,1)} %kn_ref.9, bf16[2048,512]{1,0:T(8,128)(2,1)} %vn_ref.9, bf16[2048,512]{1,0:T(8,128)(2,1)} %vn_ref.9, ...), custom_call_target="tpu_custom_call" | custom-call | flops 20000000000 | bytes 70000000 | tf_op jit(solution)/shard_map/attend/pallas_call | solution.py:236
  37.0 0.3 collective-permute-start.5
  37.2 2.4 %attend.6 = bf16[256,512]{1,0:T(8,128)(2,1)S(1)} custom-call(s32[9]{0:T(128)S(1)} %stack.39.info, bf16[2048,512]{1,0:T(8,128)(2,1)S(1)} %copy-done, bf16[2048,512]{1,0:T(8,128)(2,1)} %kn_ref.9, bf16[2048,512]{1,0:T(8,128)(2,1)} %kn_ref.9, bf16[2048,512]{1,0:T(8,128)(2,1)} %kn_ref.9, bf16[2048,512]{1,0:T(8,128)(2,1)} %vn_ref.9, bf16[2048,512]{1,0:T(8,128)(2,1)} %vn_ref.9, ...), custom_call_target="tpu_custom_call" | custom-call | flops 20000000000 | bytes 70000000 | tf_op jit(solution)/shard_map/attend/pallas_call | solution.py:236
  39.6 1.4 %collective-permute-start.6 = (bf16[256,512]{1,0:T(8,128)(2,1)S(1)}, bf16[256,512]{1,0:T(8,128)(2,1)S(1)}, u32[]{:S(2)}, u32[]{:S(2)}) collective-permute-start(bf16[256,512]{1,0:T(8,128)(2,1)S(1)} %attend.6), channel_id=1, source_target_pairs={{0,2},{1,3},{2,0},{3,1},{4,6},{5,7},{6,4},{7,5},{8,10},{9,11},{10,... | collective-permute-start | bytes 786440 | tf_op jit(solution)/shard_map/ppermute | solution.py:346
  41.0 3.7 %attend.7 = bf16[512,512]{1,0:T(8,128)(2,1)S(1)} custom-call(s32[9]{0:T(128)S(1)} %stack.39.info, bf16[2048,512]{1,0:T(8,128)(2,1)} %q_ref.9, bf16[2048,512]{1,0:T(8,128)(2,1)} %kn_ref.9, bf16[2048,512]{1,0:T(8,128)(2,1)} %kn_ref.9, bf16[2048,512]{1,0:T(8,128)(2,1)} %kn_ref.9, bf16[2048,512]{1,0:T(8,128)(2,1)} %vn_ref.9, bf16[2048,512]{1,0:T(8,128)(2,1)} %vn_ref.9, ...), custom_call_target="tpu_custom_call" | custom-call | flops 20000000000 | bytes 70000000 | tf_op jit(solution)/shard_map/attend/pallas_call | solution.py:236
  44.7 3.7 %collective-permute-start.7 = (bf16[512,512]{1,0:T(8,128)(2,1)S(1)}, bf16[512,512]{1,0:T(8,128)(2,1)S(1)}, u32[]{:S(2)}, u32[]{:S(2)}) collective-permute-start(bf16[512,512]{1,0:T(8,128)(2,1)S(1)} %attend.7), channel_id=1, source_target_pairs={{0,3},{1,2},{2,1},{3,0},{4,7},{5,6},{6,5},{7,4},{8,11},{9,10},{10,... | collective-permute-start | bytes 1572872 | tf_op jit(solution)/shard_map/ppermute | solution.py:346
  48.4 3.7 %attend.9 = bf16[512,512]{1,0:T(8,128)(2,1)S(1)} custom-call(s32[9]{0:T(128)S(1)} %stack.39.info, bf16[2048,512]{1,0:T(8,128)(2,1)} %q_ref.9, bf16[2048,512]{1,0:T(8,128)(2,1)} %kn_ref.9, bf16[2048,512]{1,0:T(8,128)(2,1)} %kn_ref.9, bf16[2048,512]{1,0:T(8,128)(2,1)} %kn_ref.9, bf16[2048,512]{1,0:T(8,128)(2,1)} %vn_ref.9, bf16[2048,512]{1,0:T(8,128)(2,1)} %vn_ref.9, ...), custom_call_target="tpu_custom_call" | custom-call | flops 20000000000 | bytes 70000000 | tf_op jit(solution)/shard_map/attend/pallas_call | solution.py:236
  52.1 0.4 collective-permute-start.8
  52.5 0.3 collective-permute-start.9
  52.7 3.7 %attend.8.refs_3_ = bf16[512,512]{1,0:T(8,128)(2,1)S(1)} custom-call(s32[9]{0:T(128)S(1)} %stack.39.info, bf16[2048,512]{1,0:T(8,128)(2,1)} %q_ref.9, bf16[2048,512]{1,0:T(8,128)(2,1)} %kn_ref.9, bf16[2048,512]{1,0:T(8,128)(2,1)} %kn_ref.9, bf16[2048,512]{1,0:T(8,128)(2,1)} %kn_ref.9, bf16[2048,512]{1,0:T(8,128)(2,1)} %vn_ref.9, bf16[2048,512]{1,0:T(8,128)(2,1)} %vn_ref.9, ...), custom_call_target="tpu_custom_call" | custom-call | flops 20000000000 | bytes 70000000 | tf_op jit(solution)/shard_map/attend/pallas_call | solution.py:236
  56.5 0.0 collective-permute-done.5.refs_4_.refs_0_
  56.5 0.0 collective-permute-done.6.refs_5_.refs_1_
  56.5 0.0 collective-permute-done.8.refs_6_
  56.5 5.8 %project.1.refs_3_ = f32[512,2048]{1,0:T(8,128)S(1)} custom-call(bf16[512,2048]{1,0:T(8,128)(2,1)} %refs_0_, bf16[512,2048]{1,0:T(8,128)(2,1)} %collective-permute-done.1.refs_1_, bf16[512,2048]{1,0:T(8,128)(2,1)} %collective-permute-done.2.refs_2_, bf16[512,512]{1,0:T(8,128)(2,1)S(1)} %attend.8.refs_3_, ...), custom_call_target="tpu_custom_call" | custom-call | flops 20000000000 | bytes 70000000 | tf_op jit(solution)/shard_map/project/pallas_call | solution.py:286
  62.3 0.0 collective-permute-done.9.refs_4_
  62.3 2.1 %finish.1 = bf16[512,2048]{1,0:T(8,128)(2,1)} custom-call(bf16[256,512]{1,0:T(8,128)(2,1)S(1)} %collective-permute-done.5.refs_4_.refs_0_, bf16[256,512]{1,0:T(8,128)(2,1)S(1)} %collective-permute-done.6.refs_5_.refs_1_, bf16[512,512]{1,0:T(8,128)(2,1)S(1)} %collective-permute-done.7.refs_2_.refs_5_, f32[512,2048]{1,0:T(8,128)S(1)} %project.1.refs_3_, ...), custom_call_target="tpu_custom_call" | custom-call | flops 20000000000 | bytes 70000000 | tf_op jit(solution)/shard_map/finish/pallas_call | solution.py:320
  (3 shorter events, 0.0 us)
Async XLA Ops:
  2.7 31.9 %copy-start = (bf16[2048,512]{1,0:T(8,128)(2,1)S(1)}, bf16[2048,512]{1,0:T(8,128)(2,1)}, u32[]{:S(2)}) copy-start(bf16[2048,512]{1,0:T(8,128)(2,1)} %q_ref.9) | copy-start | bytes 6291460
  2.7 30.8 %collective-permute-start.2 = (bf16[512,2048]{1,0:T(8,128)(2,1)}, bf16[512,2048]{1,0:T(8,128)(2,1)}, u32[]{:S(2)}, u32[]{:S(2)}) collective-permute-start(bf16[512,2048]{1,0:T(8,128)(2,1)} %refs_0_), channel_id=1, source_target_pairs={{0,1},{1,0},{2,3},{3,2},{4,5},{5,4},{6,7},{7,6},{8,9},{9,8},{10,11... | collective-permute-start | bytes 6291464 | tf_op jit(solution)/shard_map/ppermute | solution.py:346
  6.0 28.2 %collective-permute-start.1 = (bf16[512,2048]{1,0:T(8,128)(2,1)}, bf16[512,2048]{1,0:T(8,128)(2,1)}, u32[]{:S(2)}, u32[]{:S(2)}) collective-permute-start(bf16[512,2048]{1,0:T(8,128)(2,1)} %refs_0_), channel_id=1, source_target_pairs={{0,2},{1,35},{2,0},{3,33},{4,6},{5,39},{6,4},{7,37},{8,10},{9,43},... | collective-permute-start | bytes 6291464 | tf_op jit(solution)/shard_map/ppermute | solution.py:353
  7.0 4.6 %collective-permute-start = (bf16[96,512]{1,0:T(8,128)(2,1)S(1)}, bf16[96,512]{1,0:T(8,128)(2,1)S(1)}, u32[]{:S(2)}, u32[]{:S(2)}) collective-permute-start(bf16[96,512]{1,0:T(8,128)(2,1)S(1)} %get-tuple-element.17.own_ref), channel_id=1, source_target_pairs={{0,4},{4,0},{8,12},{12,8},{16,20},{20,16},{24,28},{28,24},{32,36},... | collective-permute-start | bytes 294920 | tf_op jit(solution)/shard_map/ppermute | solution.py:343
  12.2 22.3 %all-to-all-start = ((bf16[32,8,128]{2,1,0:T(8,128)(2,1)}), bf16[32,8,128]{2,1,0:T(8,128)(2,1)S(1)}, u32[]{:S(2)}, u32[]{:S(2)}) async-start(bf16[32,8,128]{2,1,0:T(8,128)(2,1)} %get-tuple-element.22), calls=%async_computation | async-start | bytes 131072 | tf_op jit(solution)/shard_map/all_to_all | solution.py:368
  23.0 10.4 %collective-permute-start.3 = (bf16[96,512]{1,0:T(8,128)(2,1)S(1)}, bf16[96,512]{1,0:T(8,128)(2,1)S(1)}, u32[]{:S(2)}, u32[]{:S(2)}) collective-permute-start(bf16[96,512]{1,0:T(8,128)(2,1)S(1)} %get-tuple-element.19.mid_ref), channel_id=1, source_target_pairs={{0,252},{4,8},{8,4},{12,16},{16,12},{20,24},{24,20},{28,32},{32,28... | collective-permute-start | bytes 294920 | tf_op jit(solution)/shard_map/ppermute | solution.py:343
  30.6 4.0 %collective-permute-start.4 = (bf16[32,512]{1,0:T(8,128)(2,1)S(1)}, bf16[32,512]{1,0:T(8,128)(2,1)S(1)}, u32[]{:S(2)}, u32[]{:S(2)}) collective-permute-start(bf16[32,512]{1,0:T(8,128)(2,1)S(1)} %slice.3), channel_id=1, source_target_pairs={{0,248},{4,12},{8,0},{12,20},{16,8},{20,28},{24,16},{28,36},{32,24... | collective-permute-start | bytes 98312 | tf_op jit(solution)/shard_map/ppermute | solution.py:343
  37.0 19.5 %collective-permute-start.5 = (bf16[256,512]{1,0:T(8,128)(2,1)S(1)}, bf16[256,512]{1,0:T(8,128)(2,1)S(1)}, u32[]{:S(2)}, u32[]{:S(2)}) collective-permute-start(bf16[256,512]{1,0:T(8,128)(2,1)S(1)} %attend.5), channel_id=1, source_target_pairs={{0,2},{1,3},{2,0},{3,1},{4,6},{5,7},{6,4},{7,5},{8,10},{9,11},{10,... | collective-permute-start | bytes 786440 | tf_op jit(solution)/shard_map/ppermute | solution.py:346
  39.6 16.9 %collective-permute-start.6 = (bf16[256,512]{1,0:T(8,128)(2,1)S(1)}, bf16[256,512]{1,0:T(8,128)(2,1)S(1)}, u32[]{:S(2)}, u32[]{:S(2)}) collective-permute-start(bf16[256,512]{1,0:T(8,128)(2,1)S(1)} %attend.6), channel_id=1, source_target_pairs={{0,2},{1,3},{2,0},{3,1},{4,6},{5,7},{6,4},{7,5},{8,10},{9,11},{10,... | collective-permute-start | bytes 786440 | tf_op jit(solution)/shard_map/ppermute | solution.py:346
  44.7 17.6 %collective-permute-start.7 = (bf16[512,512]{1,0:T(8,128)(2,1)S(1)}, bf16[512,512]{1,0:T(8,128)(2,1)S(1)}, u32[]{:S(2)}, u32[]{:S(2)}) collective-permute-start(bf16[512,512]{1,0:T(8,128)(2,1)S(1)} %attend.7), channel_id=1, source_target_pairs={{0,3},{1,2},{2,1},{3,0},{4,7},{5,6},{6,5},{7,4},{8,11},{9,10},{10,... | collective-permute-start | bytes 1572872 | tf_op jit(solution)/shard_map/ppermute | solution.py:346
  52.1 4.4 %collective-permute-start.8 = (bf16[512,512]{1,0:T(8,128)(2,1)S(1)}, bf16[512,512]{1,0:T(8,128)(2,1)S(1)}, u32[]{:S(2)}, u32[]{:S(2)}) collective-permute-start(bf16[512,512]{1,0:T(8,128)(2,1)S(1)} %attend.9), channel_id=1, source_target_pairs={{0,1},{1,0},{2,3},{3,2},{4,5},{5,4},{6,7},{7,6},{8,9},{9,8},{10,11... | collective-permute-start | bytes 1572872 | tf_op jit(solution)/shard_map/ppermute | solution.py:346
  52.5 9.8 %collective-permute-start.9 = (bf16[512,2048]{1,0:T(8,128)(2,1)}, bf16[512,2048]{1,0:T(8,128)(2,1)S(1)}, u32[]{:S(2)}, u32[]{:S(2)}) collective-permute-start(bf16[512,2048]{1,0:T(8,128)(2,1)} %collective-permute-done.1.refs_1_), channel_id=1, source_target_pairs={{0,1},{1,0},{2,3},{3,2},{4,5},{5,4},{6,7},{7,6},{8,9},{9,8},{10,11... | collective-permute-start | bytes 6291464 | tf_op jit(solution)/shard_map/ppermute | solution.py:346

commit v5 on v4

--- a/solution.py
+++ b/solution.py
@@ -116,8 +116,8 @@
 
 
 def attend_kernel(
-    total, base, info, q_ref, k_ref, kp_ref, kn_ref, v_ref, vp_ref, vn_ref, l1_ref, mid_ref, near_ref,
-    far_ref, farther_ref, l3_ref, out_ref, kx, vx, l1x, sk, sv,
+    total, base, info, q_ref, k_ref, kp_ref, kn_ref, v_ref, vp_ref, vn_ref, far_ref, l1_ref, mid_ref,
+    near_ref, farther_ref, l3_ref, out_ref, kx, vx, l1x, sk, sv,
 ):
     step = pl.program_id(0)
     block = info[0]
@@ -255,9 +255,15 @@
     )(info, *rows, *small)
 
 
-def project_kernel(ahead, n, m, *refs):
-    refs = refs[ahead:]
-    before, weights, attended, out_ref = refs[: -n - m - 1], refs[-n - m - 1 : -n - 1], refs[-n - 1 : -1], refs[-1]
+def project_kernel(n, *refs):
+    weights, attended, out_ref, tiles, sems = refs[:n], refs[n:-3], refs[-3], refs[-2], refs[-1]
+    count, depth, width = tiles.shape
+    copies = []
+    for i in range(count):
+        for j, w in enumerate(weights):
+            target = tiles.at[i, pl.ds(j * depth // n, depth // n), :]
+            copies.append(pltpu.make_async_copy(w.at[:, pl.ds(i * width, width)], target, sems.at[i, j]))
+            copies[-1].start()
     whole, halves = [], []
     for a in attended:
         if a.shape[0] == out_ref.shape[0]:
@@ -268,36 +274,30 @@
                 whole.append(jnp.concatenate(halves, axis=0))
                 halves = []
     left = jnp.concatenate(whole, axis=1)
-    right = jnp.concatenate([w[...] for w in weights], axis=0)
-    total = jnp.dot(left, right, preferred_element_type=F32)
-    if before:
-        total += before[0][...]
-    out_ref[...] = total.astype(out_ref.dtype)
-
-
-def project(attended, weights, before, dtype, ahead=()):
+    for i in range(count):
+        for copy in copies[n * i : n * i + n]:
+            copy.wait()
+        out_ref[:, width * i : width * i + width] = jnp.dot(left, tiles[i], preferred_element_type=F32)
+
+
+def project(attended, weights):
     rows, columns = attended[0].shape[0], weights[0].shape[1]
-    tile = 1024
     depth = sum(w.shape[0] for w in weights)
-
-    def tiles(arrays):
-        return [pl.BlockSpec((w.shape[0], tile), lambda i: (0, i)) for w in arrays]
-
-    return pl.pallas_call(
-        functools.partial(project_kernel, len(ahead), len(attended), len(weights)),
-        grid=(columns // tile,),
-        in_specs=[
-            *(pl.BlockSpec(memory_space=pl.ANY) for _ in ahead),
-            *tiles(before),
-            *tiles(weights),
-            *(pl.BlockSpec(a.shape, lambda i: (0, 0)) for a in attended),
-        ],
-        out_specs=pl.BlockSpec((rows, tile), lambda i: (0, i)),
-        out_shape=jax.ShapeDtypeStruct((rows, columns), dtype),
-        cost_estimate=pl.CostEstimate(flops=20000000000, bytes_accessed=70000000, transcendentals=0),
+    tiles = 4
+    return pl.pallas_call(
+        functools.partial(project_kernel, len(weights)),
+        in_specs=[pl.BlockSpec(memory_space=pl.ANY) for _ in weights]
+        + [pl.BlockSpec(memory_space=pltpu.VMEM) for _ in attended],
+        out_specs=pl.BlockSpec(memory_space=pltpu.VMEM),
+        scratch_shapes=[
+            pltpu.VMEM((tiles, depth, columns // tiles), BF16),
+            pltpu.SemaphoreType.DMA((tiles, len(weights))),
+        ],
+        out_shape=jax.ShapeDtypeStruct((rows, columns), F32),
+        cost_estimate=PROJECT_COST,
         compiler_params=pltpu.CompilerParams(vmem_limit_bytes=PROJECT_VMEM),
         name="project",
-    )(*ahead, *before, *weights, *attended)
+    )(*weights, *attended)
 
 
 def finish_kernel(ahead, *refs):
@@ -370,13 +370,13 @@
     w_far, w_near, far = lax.optimization_barrier((w_far, w_near, far))
     w_cross = swap(w_far, 1)
     rows = (queries, keys, keys, keys, values, values, values)
-    small = (l1, to_far, near, far, farther, l3)
+    small = (far, l1, to_far, near, farther, l3)
     foreign = [swap(attend(total, part, 1, info, rows, small), 2) for part in range(2)]
     last = swap(attend(total, 2, 2, info, rows, small), 3)
     inside = swap(attend(total, 4, 2, info, rows, small), 1)
     own = attend(total, 6, 2, info, rows, small)
 
-    inner = project([own, *foreign, inside], [out_weight, w_far, w_near], [], F32)
+    inner = project([own, *foreign, inside], [out_weight, w_far, w_near])
     return finish(last, w_cross, inner, [*foreign, last])
 
 

time: 64.9 us -> 64.5 us (level)
  transfers between devices with their start and end apart: 11 -> 11, of which waited for: 4 -> 4; matrix products, arithmetic and copies ran while one was open for 0% -> 0% of each run, Pallas kernels for 31% -> 30%
where the time goes in v5:
time: 64.5 us; the launch traced here: 64.2 us
  starting transfers between devices  32.4 us (50%)
  Pallas kernels  26.7 us (41%)
  waiting for transfers between devices  4.78 us (7%)
    pallas_call x5, Pallas kernels, attend(): pl.pallas_call(functools.partial(attend_kernel, total, base), grid_spec=p...  15.9 us
    ppermute x3, starting transfers between devices, permute(): lax.ppermute(array, 'seq', [(i, move(i) % blocks) for i in range(blocks)])  11.3 us
    all_to_all x1, starting transfers between devices, body(): l3 = lax.all_to_all(l3, 'seq', 0, 0, axis_index_groups=peers)  10.8 us
    ppermute x6, starting transfers between devices, swap(): return lax.ppermute(array, 'head', [(i, i ^ bit) for i in range(4)])  9.29 us
    pallas_call x1, Pallas kernels, project(): pl.pallas_call(functools.partial(project_kernel, len(weights)), in_specs=...  5.39 us
    ppermute x3, waiting for transfers between devices, permute(): lax.ppermute(array, 'seq', [(i, move(i) % blocks) for i in range(blocks)])  4.04 us
    pallas_call x1, Pallas kernels, pool(): pl.pallas_call(pool_kernel, in_specs=[pl.BlockSpec(memory_space=pltpu.HBM...  2.65 us
    pallas_call x1, Pallas kernels, finish(): pl.pallas_call(functools.partial(finish_kernel, len(ahead)), in_specs=[pl...  2.14 us
  transfers between devices with their start and end apart: 11, of which 4 were waited for; matrix products, arithmetic and copies ran while one was open for 0% of the time, Pallas kernels for 30%

profile of v5, /device:TPU:1, one launch (start us, length us, event | category | flops | bytes accessed | tf_op | source)
XLA Modules:
  0.0 64.2 jit_solution(13849840649888246164)
XLA Ops:
  0.0 2.6 %pool.1 = (bf16[2,128,512]{2,1,0:T(8,128)(2,1)S(1)}, bf16[96,512]{1,0:T(8,128)(2,1)S(1)}, bf16[64,512]{1,0:T(8,128)(2,1)S(1)}) custom-call(bf16[2048,512]{1,0:T(8,128)(2,1)} %kn_ref.9, bf16[2048,512]{1,0:T(8,128)(2,1)} %vn_ref.9), custom_call_target="tpu_custom_call" | custom-call | flops 4000000000 | bytes 14000000 | tf_op jit(solution)/shard_map/pool/pallas_call | solution.py:69
  2.7 0.0 copy-start
  2.7 3.3 %collective-permute-start.1 = (bf16[512,2048]{1,0:T(8,128)(2,1)}, bf16[512,2048]{1,0:T(8,128)(2,1)}, u32[]{:S(2)}, u32[]{:S(2)}) collective-permute-start(bf16[512,2048]{1,0:T(8,128)(2,1)} %refs_0_), channel_id=1, source_target_pairs={{0,1},{1,0},{2,3},{3,2},{4,5},{5,4},{6,7},{7,6},{8,9},{9,8},{10,11... | collective-permute-start | bytes 6291464 | tf_op jit(solution)/shard_map/ppermute | solution.py:346
  6.0 1.0 %collective-permute-start = (bf16[512,2048]{1,0:T(8,128)(2,1)}, bf16[512,2048]{1,0:T(8,128)(2,1)}, u32[]{:S(2)}, u32[]{:S(2)}) collective-permute-start(bf16[512,2048]{1,0:T(8,128)(2,1)} %refs_0_), channel_id=1, source_target_pairs={{0,2},{1,35},{2,0},{3,33},{4,6},{5,39},{6,4},{7,37},{8,10},{9,43},... | collective-permute-start | bytes 6291464 | tf_op jit(solution)/shard_map/ppermute | solution.py:353
  7.0 1.6 %collective-permute-start.2 = (bf16[96,512]{1,0:T(8,128)(2,1)S(1)}, bf16[96,512]{1,0:T(8,128)(2,1)S(1)}, u32[]{:S(2)}, u32[]{:S(2)}) collective-permute-start(bf16[96,512]{1,0:T(8,128)(2,1)S(1)} %get-tuple-element.17.own_ref), channel_id=1, source_target_pairs={{0,4},{4,0},{8,12},{12,8},{16,20},{20,16},{24,28},{28,24},{32,36},... | collective-permute-start | bytes 294920 | tf_op jit(solution)/shard_map/ppermute | solution.py:343
  8.6 3.0 %collective-permute-done.2.near_ref = bf16[96,512]{1,0:T(8,128)(2,1)S(1)} collective-permute-done((bf16[96,512]{1,0:T(8,128)(2,1)S(1)}, bf16[96,512]{1,0:T(8,128)(2,1)S(1)}, u32[]{:S(2)}, u32[]{:S(2)}) %collective-permute-start.2) | collective-permute-done | bytes 98336 | tf_op jit(solution)/shard_map/ppermute | solution.py:343
  11.6 0.7 %middle.1 = (bf16[96,512]{1,0:T(8,128)(2,1)S(1)}, bf16[32,8,128]{2,1,0:T(8,128)(2,1)}) custom-call(bf16[96,512]{1,0:T(8,128)(2,1)S(1)} %get-tuple-element.17.own_ref, bf16[96,512]{1,0:T(8,128)(2,1)S(1)} %collective-permute-done.2.near_ref, bf16[64,512]{1,0:T(8,128)(2,1)S(1)} %get-tuple-element.18.far_ref), custom_call_target="tpu_custom_call" | custom-call | flops 1000000000 | bytes 3500000 | tf_op jit(solution)/shard_map/middle/pallas_call | solution.py:106
  12.2 10.8 %all-to-all-start = ((bf16[32,8,128]{2,1,0:T(8,128)(2,1)}), bf16[32,8,128]{2,1,0:T(8,128)(2,1)S(1)}, u32[]{:S(2)}, u32[]{:S(2)}) async-start(bf16[32,8,128]{2,1,0:T(8,128)(2,1)} %get-tuple-element.22), calls=%async_computation | async-start | bytes 131072 | tf_op jit(solution)/shard_map/all_to_all | solution.py:368
  23.0 7.6 %collective-permute-start.3 = (bf16[96,512]{1,0:T(8,128)(2,1)S(1)}, bf16[96,512]{1,0:T(8,128)(2,1)S(1)}, u32[]{:S(2)}, u32[]{:S(2)}) collective-permute-start(bf16[96,512]{1,0:T(8,128)(2,1)S(1)} %get-tuple-element.19.mid_ref), channel_id=1, source_target_pairs={{0,252},{4,8},{8,4},{12,16},{16,12},{20,24},{24,20},{28,32},{32,28... | collective-permute-start | bytes 294920 | tf_op jit(solution)/shard_map/ppermute | solution.py:343
  30.6 2.1 %collective-permute-start.4 = (bf16[32,512]{1,0:T(8,128)(2,1)S(1)}, bf16[32,512]{1,0:T(8,128)(2,1)S(1)}, u32[]{:S(2)}, u32[]{:S(2)}) collective-permute-start(bf16[32,512]{1,0:T(8,128)(2,1)S(1)} %slice.3), channel_id=1, source_target_pairs={{0,248},{4,12},{8,0},{12,20},{16,8},{20,28},{24,16},{28,36},{32,24... | collective-permute-start | bytes 98312 | tf_op jit(solution)/shard_map/ppermute | solution.py:343
  32.7 0.1 stack.39.info
  32.8 0.7 %collective-permute-done.3.far_ref = bf16[96,512]{1,0:T(8,128)(2,1)S(1)} collective-permute-done((bf16[96,512]{1,0:T(8,128)(2,1)S(1)}, bf16[96,512]{1,0:T(8,128)(2,1)S(1)}, u32[]{:S(2)}, u32[]{:S(2)}) %collective-permute-start.3) | collective-permute-done | bytes 98336 | tf_op jit(solution)/shard_map/ppermute | solution.py:343
  33.4 0.0 collective-permute-done.1.refs_2_
  33.4 0.7 %collective-permute-done.refs_1_ = bf16[512,2048]{1,0:T(8,128)(2,1)} collective-permute-done((bf16[512,2048]{1,0:T(8,128)(2,1)}, bf16[512,2048]{1,0:T(8,128)(2,1)}, u32[]{:S(2)}, u32[]{:S(2)}) %collective-permute-start) | collective-permute-done | bytes 2097184 | tf_op jit(solution)/shard_map/ppermute | solution.py:353
  34.2 0.4 collective-permute-done.4.farther_ref
  34.6 0.0 all-to-all-done.l3_ref
  34.6 2.4 %attend.5 = bf16[256,512]{1,0:T(8,128)(2,1)S(1)} custom-call(s32[9]{0:T(128)S(1)} %stack.39.info, bf16[2048,512]{1,0:T(8,128)(2,1)S(1)} %copy-done, bf16[2048,512]{1,0:T(8,128)(2,1)} %kn_ref.9, bf16[2048,512]{1,0:T(8,128)(2,1)} %kn_ref.9, bf16[2048,512]{1,0:T(8,128)(2,1)} %kn_ref.9, bf16[2048,512]{1,0:T(8,128)(2,1)} %vn_ref.9, bf16[2048,512]{1,0:T(8,128)(2,1)} %vn_ref.9, ...), custom_call_target="tpu_custom_call" | custom-call | flops 20000000000 | bytes 70000000 | tf_op jit(solution)/shard_map/attend/pallas_call | solution.py:236
  37.0 0.3 collective-permute-start.5
  37.2 2.4 %attend.6 = bf16[256,512]{1,0:T(8,128)(2,1)S(1)} custom-call(s32[9]{0:T(128)S(1)} %stack.39.info, bf16[2048,512]{1,0:T(8,128)(2,1)S(1)} %copy-done, bf16[2048,512]{1,0:T(8,128)(2,1)} %kn_ref.9, bf16[2048,512]{1,0:T(8,128)(2,1)} %kn_ref.9, bf16[2048,512]{1,0:T(8,128)(2,1)} %kn_ref.9, bf16[2048,512]{1,0:T(8,128)(2,1)} %vn_ref.9, bf16[2048,512]{1,0:T(8,128)(2,1)} %vn_ref.9, ...), custom_call_target="tpu_custom_call" | custom-call | flops 20000000000 | bytes 70000000 | tf_op jit(solution)/shard_map/attend/pallas_call | solution.py:236
  39.6 1.4 %collective-permute-start.6 = (bf16[256,512]{1,0:T(8,128)(2,1)S(1)}, bf16[256,512]{1,0:T(8,128)(2,1)S(1)}, u32[]{:S(2)}, u32[]{:S(2)}) collective-permute-start(bf16[256,512]{1,0:T(8,128)(2,1)S(1)} %attend.6), channel_id=1, source_target_pairs={{0,2},{1,3},{2,0},{3,1},{4,6},{5,7},{6,4},{7,5},{8,10},{9,11},{10,... | collective-permute-start | bytes 786440 | tf_op jit(solution)/shard_map/ppermute | solution.py:346
  41.0 3.7 %attend.7 = bf16[512,512]{1,0:T(8,128)(2,1)S(1)} custom-call(s32[9]{0:T(128)S(1)} %stack.39.info, bf16[2048,512]{1,0:T(8,128)(2,1)} %q_ref.9, bf16[2048,512]{1,0:T(8,128)(2,1)} %kn_ref.9, bf16[2048,512]{1,0:T(8,128)(2,1)} %kn_ref.9, bf16[2048,512]{1,0:T(8,128)(2,1)} %kn_ref.9, bf16[2048,512]{1,0:T(8,128)(2,1)} %vn_ref.9, bf16[2048,512]{1,0:T(8,128)(2,1)} %vn_ref.9, ...), custom_call_target="tpu_custom_call" | custom-call | flops 20000000000 | bytes 70000000 | tf_op jit(solution)/shard_map/attend/pallas_call | solution.py:236
  44.7 3.7 %collective-permute-start.7 = (bf16[512,512]{1,0:T(8,128)(2,1)S(1)}, bf16[512,512]{1,0:T(8,128)(2,1)S(1)}, u32[]{:S(2)}, u32[]{:S(2)}) collective-permute-start(bf16[512,512]{1,0:T(8,128)(2,1)S(1)} %attend.7), channel_id=1, source_target_pairs={{0,3},{1,2},{2,1},{3,0},{4,7},{5,6},{6,5},{7,4},{8,11},{9,10},{10,... | collective-permute-start | bytes 1572872 | tf_op jit(solution)/shard_map/ppermute | solution.py:346
  48.4 3.7 %attend.9 = bf16[512,512]{1,0:T(8,128)(2,1)S(1)} custom-call(s32[9]{0:T(128)S(1)} %stack.39.info, bf16[2048,512]{1,0:T(8,128)(2,1)} %q_ref.9, bf16[2048,512]{1,0:T(8,128)(2,1)} %kn_ref.9, bf16[2048,512]{1,0:T(8,128)(2,1)} %kn_ref.9, bf16[2048,512]{1,0:T(8,128)(2,1)} %kn_ref.9, bf16[2048,512]{1,0:T(8,128)(2,1)} %vn_ref.9, bf16[2048,512]{1,0:T(8,128)(2,1)} %vn_ref.9, ...), custom_call_target="tpu_custom_call" | custom-call | flops 20000000000 | bytes 70000000 | tf_op jit(solution)/shard_map/attend/pallas_call | solution.py:236
  52.1 0.4 collective-permute-start.8
  52.5 0.3 collective-permute-start.9
  52.7 3.7 %attend.8.refs_3_ = bf16[512,512]{1,0:T(8,128)(2,1)S(1)} custom-call(s32[9]{0:T(128)S(1)} %stack.39.info, bf16[2048,512]{1,0:T(8,128)(2,1)} %q_ref.9, bf16[2048,512]{1,0:T(8,128)(2,1)} %kn_ref.9, bf16[2048,512]{1,0:T(8,128)(2,1)} %kn_ref.9, bf16[2048,512]{1,0:T(8,128)(2,1)} %kn_ref.9, bf16[2048,512]{1,0:T(8,128)(2,1)} %vn_ref.9, bf16[2048,512]{1,0:T(8,128)(2,1)} %vn_ref.9, ...), custom_call_target="tpu_custom_call" | custom-call | flops 20000000000 | bytes 70000000 | tf_op jit(solution)/shard_map/attend/pallas_call | solution.py:236
  56.5 0.0 collective-permute-done.5.refs_4_.refs_0_
  56.5 0.0 collective-permute-done.6.refs_5_.refs_1_
  56.5 0.0 collective-permute-done.8.refs_6_
  56.5 5.4 %project.1.refs_3_ = f32[512,2048]{1,0:T(8,128)S(1)} custom-call(bf16[512,2048]{1,0:T(8,128)(2,1)} %refs_0_, bf16[512,2048]{1,0:T(8,128)(2,1)} %collective-permute-done.refs_1_, bf16[512,2048]{1,0:T(8,128)(2,1)} %collective-permute-done.1.refs_2_, bf16[512,512]{1,0:T(8,128)(2,1)S(1)} %attend.8.refs_3_, ...), custom_call_target="tpu_custom_call" | custom-call | flops 20000000000 | bytes 70000000 | tf_op jit(solution)/shard_map/project/pallas_call | solution.py:287
  61.9 0.0 collective-permute-done.7.refs_2_.refs_5_
  61.9 2.1 %finish.1 = bf16[512,2048]{1,0:T(8,128)(2,1)} custom-call(bf16[256,512]{1,0:T(8,128)(2,1)S(1)} %collective-permute-done.5.refs_4_.refs_0_, bf16[256,512]{1,0:T(8,128)(2,1)S(1)} %collective-permute-done.6.refs_5_.refs_1_, bf16[512,512]{1,0:T(8,128)(2,1)S(1)} %collective-permute-done.7.refs_2_.refs_5_, f32[512,2048]{1,0:T(8,128)S(1)} %project.1.refs_3_, ...), custom_call_target="tpu_custom_call" | custom-call | flops 20000000000 | bytes 70000000 | tf_op jit(solution)/shard_map/finish/pallas_call | solution.py:320
  (3 shorter events, 0.0 us)
Async XLA Ops:
  2.7 31.9 %copy-start = (bf16[2048,512]{1,0:T(8,128)(2,1)S(1)}, bf16[2048,512]{1,0:T(8,128)(2,1)}, u32[]{:S(2)}) copy-start(bf16[2048,512]{1,0:T(8,128)(2,1)} %q_ref.9) | copy-start | bytes 6291460
  2.7 30.8 %collective-permute-start.1 = (bf16[512,2048]{1,0:T(8,128)(2,1)}, bf16[512,2048]{1,0:T(8,128)(2,1)}, u32[]{:S(2)}, u32[]{:S(2)}) collective-permute-start(bf16[512,2048]{1,0:T(8,128)(2,1)} %refs_0_), channel_id=1, source_target_pairs={{0,1},{1,0},{2,3},{3,2},{4,5},{5,4},{6,7},{7,6},{8,9},{9,8},{10,11... | collective-permute-start | bytes 6291464 | tf_op jit(solution)/shard_map/ppermute | solution.py:346
  6.0 28.2 %collective-permute-start = (bf16[512,2048]{1,0:T(8,128)(2,1)}, bf16[512,2048]{1,0:T(8,128)(2,1)}, u32[]{:S(2)}, u32[]{:S(2)}) collective-permute-start(bf16[512,2048]{1,0:T(8,128)(2,1)} %refs_0_), channel_id=1, source_target_pairs={{0,2},{1,35},{2,0},{3,33},{4,6},{5,39},{6,4},{7,37},{8,10},{9,43},... | collective-permute-start | bytes 6291464 | tf_op jit(solution)/shard_map/ppermute | solution.py:353
  7.0 4.6 %collective-permute-start.2 = (bf16[96,512]{1,0:T(8,128)(2,1)S(1)}, bf16[96,512]{1,0:T(8,128)(2,1)S(1)}, u32[]{:S(2)}, u32[]{:S(2)}) collective-permute-start(bf16[96,512]{1,0:T(8,128)(2,1)S(1)} %get-tuple-element.17.own_ref), channel_id=1, source_target_pairs={{0,4},{4,0},{8,12},{12,8},{16,20},{20,16},{24,28},{28,24},{32,36},... | collective-permute-start | bytes 294920 | tf_op jit(solution)/shard_map/ppermute | solution.py:343
  12.2 22.3 %all-to-all-start = ((bf16[32,8,128]{2,1,0:T(8,128)(2,1)}), bf16[32,8,128]{2,1,0:T(8,128)(2,1)S(1)}, u32[]{:S(2)}, u32[]{:S(2)}) async-start(bf16[32,8,128]{2,1,0:T(8,128)(2,1)} %get-tuple-element.22), calls=%async_computation | async-start | bytes 131072 | tf_op jit(solution)/shard_map/all_to_all | solution.py:368
  23.0 10.4 %collective-permute-start.3 = (bf16[96,512]{1,0:T(8,128)(2,1)S(1)}, bf16[96,512]{1,0:T(8,128)(2,1)S(1)}, u32[]{:S(2)}, u32[]{:S(2)}) collective-permute-start(bf16[96,512]{1,0:T(8,128)(2,1)S(1)} %get-tuple-element.19.mid_ref), channel_id=1, source_target_pairs={{0,252},{4,8},{8,4},{12,16},{16,12},{20,24},{24,20},{28,32},{32,28... | collective-permute-start | bytes 294920 | tf_op jit(solution)/shard_map/ppermute | solution.py:343
  30.6 4.0 %collective-permute-start.4 = (bf16[32,512]{1,0:T(8,128)(2,1)S(1)}, bf16[32,512]{1,0:T(8,128)(2,1)S(1)}, u32[]{:S(2)}, u32[]{:S(2)}) collective-permute-start(bf16[32,512]{1,0:T(8,128)(2,1)S(1)} %slice.3), channel_id=1, source_target_pairs={{0,248},{4,12},{8,0},{12,20},{16,8},{20,28},{24,16},{28,36},{32,24... | collective-permute-start | bytes 98312 | tf_op jit(solution)/shard_map/ppermute | solution.py:343
  37.0 19.5 %collective-permute-start.5 = (bf16[256,512]{1,0:T(8,128)(2,1)S(1)}, bf16[256,512]{1,0:T(8,128)(2,1)S(1)}, u32[]{:S(2)}, u32[]{:S(2)}) collective-permute-start(bf16[256,512]{1,0:T(8,128)(2,1)S(1)} %attend.5), channel_id=1, source_target_pairs={{0,2},{1,3},{2,0},{3,1},{4,6},{5,7},{6,4},{7,5},{8,10},{9,11},{10,... | collective-permute-start | bytes 786440 | tf_op jit(solution)/shard_map/ppermute | solution.py:346
  39.6 16.9 %collective-permute-start.6 = (bf16[256,512]{1,0:T(8,128)(2,1)S(1)}, bf16[256,512]{1,0:T(8,128)(2,1)S(1)}, u32[]{:S(2)}, u32[]{:S(2)}) collective-permute-start(bf16[256,512]{1,0:T(8,128)(2,1)S(1)} %attend.6), channel_id=1, source_target_pairs={{0,2},{1,3},{2,0},{3,1},{4,6},{5,7},{6,4},{7,5},{8,10},{9,11},{10,... | collective-permute-start | bytes 786440 | tf_op jit(solution)/shard_map/ppermute | solution.py:346
  44.7 17.2 %collective-permute-start.7 = (bf16[512,512]{1,0:T(8,128)(2,1)S(1)}, bf16[512,512]{1,0:T(8,128)(2,1)S(1)}, u32[]{:S(2)}, u32[]{:S(2)}) collective-permute-start(bf16[512,512]{1,0:T(8,128)(2,1)S(1)} %attend.7), channel_id=1, source_target_pairs={{0,3},{1,2},{2,1},{3,0},{4,7},{5,6},{6,5},{7,4},{8,11},{9,10},{10,... | collective-permute-start | bytes 1572872 | tf_op jit(solution)/shard_map/ppermute | solution.py:346
  52.1 4.4 %collective-permute-start.8 = (bf16[512,512]{1,0:T(8,128)(2,1)S(1)}, bf16[512,512]{1,0:T(8,128)(2,1)S(1)}, u32[]{:S(2)}, u32[]{:S(2)}) collective-permute-start(bf16[512,512]{1,0:T(8,128)(2,1)S(1)} %attend.9), channel_id=1, source_target_pairs={{0,1},{1,0},{2,3},{3,2},{4,5},{5,4},{6,7},{7,6},{8,9},{9,8},{10,11... | collective-permute-start | bytes 1572872 | tf_op jit(solution)/shard_map/ppermute | solution.py:346
  52.5 9.5 %collective-permute-start.9 = (bf16[512,2048]{1,0:T(8,128)(2,1)}, bf16[512,2048]{1,0:T(8,128)(2,1)S(1)}, u32[]{:S(2)}, u32[]{:S(2)}) collective-permute-start(bf16[512,2048]{1,0:T(8,128)(2,1)} %collective-permute-done.refs_1_), channel_id=1, source_target_pairs={{0,1},{1,0},{2,3},{3,2},{4,5},{5,4},{6,7},{7,6},{8,9},{9,8},{10,11... | collective-permute-start | bytes 6291464 | tf_op jit(solution)/shard_map/ppermute | solution.py:346
